TPU v7x, 128 devices: a whole 4x4x4 slice. The times are simulated.
128 devices in a mesh: row: 64 (over y, x, z), col: 2 (over core).
Axes of the slice: x: 4, y: 4, z: 4, core: 2. Of those that a mesh axis runs over, the one named last changes fastest.
Arguments:
- pair_rep: bfloat16 [2048, 256, 128], P('row', 'col'), may hold values from -6 to 6
- token_counts: int32 [16], replicated, may hold values from 64 to 256, as said below
- first_device: int32 [16], replicated, may hold values from 0 to 62, as said below
- norm_gain: float32 [2, 2, 128], replicated, may hold values from 0.1 to 1.9
- norm_bias: float32 [2, 2, 128], replicated, may hold values from -3 to 3
- proj_weight: bfloat16 [2, 128, 512], replicated, may hold values from -0.5 to 0.5
- gate_weight: bfloat16 [2, 128, 128], replicated, may hold values from -0.5 to 0.5
- out_weight: bfloat16 [2, 128, 128], replicated, may hold values from -0.5 to 0.5
Outputs:
- updated: bfloat16 [2048, 256, 128], P('row', 'col')
Inputs may be any that keep to these rules, and one draw needn't show every extreme that they name: Each complex occupies token_counts / 32 consecutive row devices, from 2 to 8; the complexes fill the row axis end to end in order. `first_device`: the sum of the earlier complexes' token counts divided by 32.
All inputs are finite; a program needn't handle non-finite values.
Results may differ from a plain program's by a relative error of at most 0.0065.
Values may be sent and summed in bfloat16 or wider, within the bound.
A program may use at most 128 MiB of HBM per device.

v0:
```python
import jax
import jax.numpy as jnp
from jax import lax
from jax.sharding import PartitionSpec as P

G_MAX = 8


EPS = 1e-05


def from_partner(block, axis, bit):
    count = lax.axis_size(axis)
    route = []
    for low in range(count):
        high = low | 1 << bit
        if high != low and high < count:
            route += [(low, high), (high, low)]
    return lax.ppermute(block, axis, route)


def shifted(value, axis, by):
    count = lax.axis_size(axis)
    pairs = [(i, i + by) for i in range(count) if 0 <= i + by < count]
    return lax.ppermute(value, axis, pairs)


def layer_norm(values, scale_mul, shift_add):
    average = jnp.mean(values, axis=-1, keepdims=True)
    centred = values - average
    variance = jnp.mean(centred * centred, axis=-1, keepdims=True)
    return centred * lax.rsqrt(variance + EPS) * scale_mul + shift_add


def project(slab, slot_mask, layer_no, norm_gain, norm_bias, proj_weight, gate_weight):
    slab_rows, slot_count, channels = slab.shape
    z_float = slab.astype(jnp.float32)
    z_normed = layer_norm(z_float, norm_gain[layer_no, 0], norm_bias[layer_no, 0]).astype(
        jnp.bfloat16
    )
    flat = z_normed.reshape(-1, channels)
    projected = jnp.dot(flat, proj_weight[layer_no], preferred_element_type=jnp.float32)
    projected = projected.reshape(slab_rows, slot_count, 4 * channels)
    left_side = (
        jax.nn.sigmoid(projected[..., :channels])
        * projected[..., channels : 2 * channels]
        * slot_mask
    ).astype(jnp.bfloat16)
    right_side = (
        jax.nn.sigmoid(projected[..., 2 * channels : 3 * channels])
        * projected[..., 3 * channels :]
        * slot_mask
    ).astype(jnp.bfloat16)
    gating = jax.nn.sigmoid(
        jnp.dot(flat, gate_weight[layer_no], preferred_element_type=jnp.float32)
    )
    return (z_float, left_side, right_side, gating.reshape(slab_rows, slot_count, channels))


def finish(z_float, summed, gating, slot_mask, layer_no, norm_gain, norm_bias, out_weight):
    slab_rows, slot_count, channels = summed.shape
    normed_sum = layer_norm(summed, norm_gain[layer_no, 1], norm_bias[layer_no, 1]).astype(
        jnp.bfloat16
    )
    update = jnp.dot(
        normed_sum.reshape(-1, channels), out_weight[layer_no], preferred_element_type=jnp.float32
    )
    update = update.reshape(slab_rows, slot_count, channels)
    return ((z_float + gating * update) * slot_mask).astype(jnp.bfloat16)


def body(
    pair_rep, token_counts, first_device, norm_gain, norm_bias, proj_weight, gate_weight, out_weight
):
    slab_rows, slot_count, channels = pair_rep.shape
    span_max = G_MAX
    half_rows = slab_rows // 2
    row_index = lax.axis_index("row")
    col_index = lax.axis_index("col")
    member = jnp.sum((first_device <= row_index).astype(jnp.int32)) - 1
    begin_dev = first_device[member]
    extent = token_counts[member] // slab_rows
    position = row_index - begin_dev
    slot_mask = (jnp.arange(slot_count) // half_rows < extent).astype(jnp.float32)[None, :, None]
    leading = col_index == 0
    offsets = [step for step in range(1, span_max)] + [-step for step in range(1, span_max)]
    z_float, left_side, right_side, gating = project(
        pair_rep, slot_mask, 0, norm_gain, norm_bias, proj_weight, gate_weight
    )
    partner_left, partner_right = from_partner((left_side, right_side), "col", 0)
    left_full = jnp.where(
        leading,
        jnp.concatenate([left_side, partner_left], 1),
        jnp.concatenate([partner_left, left_side], 1),
    )
    right_full = jnp.where(
        leading,
        jnp.concatenate([right_side, partner_right], 1),
        jnp.concatenate([partner_right, right_side], 1),
    )
    right_rows = lax.dynamic_slice_in_dim(right_full, col_index * half_rows, half_rows, 0)
    segments = [(0, right_rows)]
    for offset in offsets:
        segments.append((offset, shifted(right_rows, "row", offset)))
    summed = jnp.zeros((slab_rows, span_max, half_rows, channels), jnp.float32)
    for offset, segment in segments:
        source = position - offset
        usable = ((source >= 0) & (source < extent)).astype(jnp.float32)
        product = jnp.einsum("ikc,ukc->iuc", left_full, segment, preferred_element_type=jnp.float32)
        slot_no = jnp.clip(source, 0, span_max - 1)
        current = lax.dynamic_slice_in_dim(summed, slot_no, 1, 1)
        summed = lax.dynamic_update_slice_in_dim(
            summed, current + usable * product[:, None], slot_no, 1
        )
    summed = summed.reshape(slab_rows, slot_count, channels)
    first_layer = finish(z_float, summed, gating, slot_mask, 0, norm_gain, norm_bias, out_weight)
    z_second, left_two, right_two, gating_two = project(
        first_layer, slot_mask, 1, norm_gain, norm_bias, proj_weight, gate_weight
    )
    partner_two = from_partner(left_two, "col", 0)
    left_pair = jnp.where(
        leading, jnp.stack([left_two, partner_two], 1), jnp.stack([partner_two, left_two], 1)
    )

    def column_block(offset):
        block_no = jnp.clip(position + offset, 0, span_max - 1)
        selected = lax.dynamic_slice_in_dim(left_pair, block_no * half_rows, half_rows, 2)
        return selected.reshape(slab_rows, slab_rows, channels)

    summed_two = jnp.einsum(
        "kic,kjc->ijc", column_block(0), right_two, preferred_element_type=jnp.float32
    )
    for offset in offsets:
        got_left, got_right = shifted((column_block(offset), right_two), "row", offset)
        source = position - offset
        usable = ((source >= 0) & (source < extent)).astype(jnp.float32)
        summed_two = summed_two + usable * jnp.einsum(
            "kic,kjc->ijc", got_left, got_right, preferred_element_type=jnp.float32
        )
    return finish(z_second, summed_two, gating_two, slot_mask, 1, norm_gain, norm_bias, out_weight)


def solution(mesh):
    return jax.shard_map(
        body,
        mesh=mesh,
        in_specs=(P("row", "col", None), P(), P(), P(), P(), P(), P(), P()),
        out_specs=P("row", "col", None),
        check_vma=False,
    )
```

profile of v0, /device:TPU:16, one launch (start us, length us, event | category | flops | bytes accessed | tf_op | source)
XLA Modules:
  0.0 940.7 jit_solution(12097720170139344572)
XLA Ops:
  19.7 2.9 fusion.43
  22.6 3.4 collective-permute-start.5
  28.0 5.9 collective-permute-start.4
  36.7 3.2 collective-permute-start.2
  42.6 4.8 collective-permute-start.6
  47.4 3.7 maximum_select_fusion
  51.1 3.4 copy.210
  61.3 4.6 collective-permute-start.7
  71.5 5.3 collective-permute-done.4
  84.6 42.9 %collective-permute-done.3 = bf16[16,256,128]{2,1,0:T(8,128)(2,1)} collective-permute-done((bf16[16,256,128]{2,1,0:T(8,128)(2,1)}, bf16[16,256,128]{2,1,0:T(8,128)(2,1)}, u32[]{:S(2)}, u32[]{:S(2)}) %collective-permute-start.3) | collective-permute-done | bytes 1048608 | tf_op jit(solution)/shard_map/ppermute | solution.py:25
  132.1 2.9 fusion.77
  135.1 13.6 %collective-permute-done.2 = bf16[16,256,128]{2,1,0:T(8,128)(2,1)} collective-permute-done((bf16[16,256,128]{2,1,0:T(8,128)(2,1)}, bf16[16,256,128]{2,1,0:T(8,128)(2,1)}, u32[]{:S(2)}, u32[]{:S(2)}) %collective-permute-start.2) | collective-permute-done | bytes 1048608 | tf_op jit(solution)/shard_map/ppermute | solution.py:25
  148.6 24.5 %collective-permute-start.10 = (bf16[16,256,128]{2,1,0:T(8,128)(2,1)}, bf16[16,256,128]{2,1,0:T(8,128)(2,1)}, u32[]{:S(2)}, u32[]{:S(2)}) collective-permute-start(bf16[16,256,128]{2,1,0:T(8,128)(2,1)} %fusion.43), channel_id=1, source_target_pairs={{4,0},{6,2},{8,4},{10,6},{12,8},{14,10},{16,12},{18,14},{20,16},{2... | collective-permute-start | bytes 3145736 | tf_op jit(solution)/shard_map/ppermute | solution.py:25
  178.7 27.6 %collective-permute-done.6 = bf16[16,256,128]{2,1,0:T(8,128)(2,1)} collective-permute-done((bf16[16,256,128]{2,1,0:T(8,128)(2,1)}, bf16[16,256,128]{2,1,0:T(8,128)(2,1)}, u32[]{:S(2)}, u32[]{:S(2)}) %collective-permute-start.6) | collective-permute-done | bytes 1048608 | tf_op jit(solution)/shard_map/ppermute | solution.py:25
  221.1 30.7 %collective-permute-start.13 = (bf16[16,256,128]{2,1,0:T(8,128)(2,1)}, bf16[16,256,128]{2,1,0:T(8,128)(2,1)}, u32[]{:S(2)}, u32[]{:S(2)}) collective-permute-start(bf16[16,256,128]{2,1,0:T(8,128)(2,1)} %fusion.43), channel_id=1, source_target_pairs={{10,0},{12,2},{14,4},{16,6},{18,8},{20,10},{22,12},{24,14},{26,16}... | collective-permute-start | bytes 3145736 | tf_op jit(solution)/shard_map/ppermute | solution.py:25
  264.7 39.1 %collective-permute-start.15 = (bf16[16,256,128]{2,1,0:T(8,128)(2,1)}, bf16[16,256,128]{2,1,0:T(8,128)(2,1)}, u32[]{:S(2)}, u32[]{:S(2)}) collective-permute-start(bf16[16,256,128]{2,1,0:T(8,128)(2,1)} %fusion.43), channel_id=1, source_target_pairs={{14,0},{16,2},{18,4},{20,6},{22,8},{24,10},{26,12},{28,14},{30,16}... | collective-permute-start | bytes 3145736 | tf_op jit(solution)/shard_map/ppermute | solution.py:25
  348.4 2.9 fusion.87
  398.5 3.3 add_convert_fusion.1
  414.8 4.4 collective-permute-start.23
  422.2 41.0 %collective-permute-done.17 = bf16[32,128,128]{2,1,0:T(8,128)(2,1)} collective-permute-done((bf16[32,128,128]{2,1,0:T(8,128)(2,1)}, bf16[32,128,128]{2,1,0:T(8,128)(2,1)}, u32[]{:S(2)}, u32[]{:S(2)}) %collective-permute-start.17) | collective-permute-done | bytes 1048608 | tf_op jit(solution)/shard_map/ppermute | solution.py:25
  465.1 56.5 %collective-permute-done.19 = bf16[32,128,128]{2,1,0:T(8,128)(2,1)} collective-permute-done((bf16[32,128,128]{2,1,0:T(8,128)(2,1)}, bf16[32,128,128]{2,1,0:T(8,128)(2,1)}, u32[]{:S(2)}, u32[]{:S(2)}) %collective-permute-start.19) | collective-permute-done | bytes 1048608 | tf_op jit(solution)/shard_map/ppermute | solution.py:25
  523.5 3.4 collective-permute-start.31
  526.9 57.2 %collective-permute-start.33 = (bf16[32,128,128]{2,1,0:T(8,128)(2,1)}, bf16[32,128,128]{2,1,0:T(8,128)(2,1)}, u32[]{:S(2)}, u32[]{:S(2)}) collective-permute-start(bf16[32,128,128]{2,1,0:T(8,128)(2,1)} %get-tuple-element.5), channel_id=1, source_target_pairs={{4,0},{6,2},{8,4},{10,6},{12,8},{14,10},{16,12},{18,14},{20,16},{2... | collective-permute-start | bytes 3145736 | tf_op jit(solution)/shard_map/ppermute | solution.py:25
  584.1 39.6 %collective-permute-done.25 = bf16[32,128,128]{2,1,0:T(8,128)(2,1)} collective-permute-done((bf16[32,128,128]{2,1,0:T(8,128)(2,1)}, bf16[32,128,128]{2,1,0:T(8,128)(2,1)}, u32[]{:S(2)}, u32[]{:S(2)}) %collective-permute-start.25) | collective-permute-done | bytes 1048608 | tf_op jit(solution)/shard_map/ppermute | solution.py:25
  627.6 42.2 %collective-permute-start.39 = (bf16[32,128,128]{2,1,0:T(8,128)(2,1)}, bf16[32,128,128]{2,1,0:T(8,128)(2,1)}, u32[]{:S(2)}, u32[]{:S(2)}) collective-permute-start(bf16[32,128,128]{2,1,0:T(8,128)(2,1)} %get-tuple-element.5), channel_id=1, source_target_pairs={{10,0},{12,2},{14,4},{16,6},{18,8},{20,10},{22,12},{24,14},{26,16}... | collective-permute-start | bytes 3145736 | tf_op jit(solution)/shard_map/ppermute | solution.py:25
  669.8 5.9 collective-permute-start.41
  677.7 3.1 copy.255
  686.7 3.6 copy.256
  736.7 6.8 collective-permute-start.22
  746.2 6.8 collective-permute-done.41
  757.6 18.3 %collective-permute-done.43 = bf16[32,128,128]{2,1,0:T(8,128)(2,1)} collective-permute-done((bf16[32,128,128]{2,1,0:T(8,128)(2,1)}, bf16[32,128,128]{2,1,0:T(8,128)(2,1)}, u32[]{:S(2)}, u32[]{:S(2)}) %collective-permute-start.43) | collective-permute-done | bytes 1048608 | tf_op jit(solution)/shard_map/ppermute | solution.py:25
  784.5 3.6 copy.259
  788.0 3.3 fusion.91
  793.3 3.6 copy.262
  796.8 3.3 fusion.92
  800.2 11.4 %collective-permute-start.32 = (bf16[32,32,128]{2,1,0:T(8,128)(2,1)}, bf16[32,32,128]{2,1,0:T(8,128)(2,1)}, u32[]{:S(2)}, u32[]{:S(2)}) collective-permute-start(bf16[32,32,128]{2,1,0:T(8,128)(2,1)} %bitcast.61), channel_id=1, source_target_pairs={{2,0},{4,2},{6,4},{8,6},{10,8},{12,10},{14,12},{16,14},{18,16},{20... | collective-permute-start | bytes 786440 | tf_op jit(solution)/shard_map/ppermute | solution.py:25
  811.6 3.6 copy.265
  815.2 3.4 fusion.93
  818.5 4.6 collective-permute-start.34
  823.2 3.6 copy.268
  826.7 3.3 fusion.94
  830.0 3.1 collective-permute-start.36
  835.7 3.4 fusion.95
  839.1 3.9 collective-permute-start.38
  843.0 3.6 copy.274
  846.6 3.3 fusion.96
  849.8 6.6 collective-permute-start.40
  856.4 3.6 copy.277
  860.0 3.2 fusion.97
  863.2 10.1 %collective-permute-start.42 = (bf16[32,32,128]{2,1,0:T(8,128)(2,1)}, bf16[32,32,128]{2,1,0:T(8,128)(2,1)}, u32[]{:S(2)}, u32[]{:S(2)}) collective-permute-start(bf16[32,32,128]{2,1,0:T(8,128)(2,1)} %bitcast.66), channel_id=1, source_target_pairs={{12,0},{14,2},{16,4},{18,6},{20,8},{22,10},{24,12},{26,14},{28,16}... | collective-permute-start | bytes 786440 | tf_op jit(solution)/shard_map/ppermute | solution.py:25
  873.3 3.6 copy.280
  876.8 3.3 fusion.98
  880.1 7.8 collective-permute-start.44
  888.0 3.6 copy.283
  891.5 3.3 fusion.99
  894.8 3.6 copy.286
  898.4 3.3 fusion.100
  904.3 3.4 fusion.101
  907.7 3.6 copy.292
  911.2 3.3 fusion.102
  914.5 3.6 copy.295
  918.1 3.4 fusion.103
  921.5 3.6 copy.298
  925.0 11.5 %bitcast_reduce_fusion = (f32[32,128]{1,0:T(8,128)S(1)}, f32[128,128,32]{1,2,0:T(8,128)S(1)}) fusion(bf16[32,32,128]{0,1,2:T(8,128)(2,1)} %copy.298, bf16[32,128,128]{1,0,2:T(8,128)(2,1)} %copy.297, f32[]{:T(128)S(6)} %convert_element_type.134, f32[128,128,32]{1,2,0:T(8,128)} %fusion.103, f32[]{:T(128)S(6)} %convert_element_type.133, ...), kind=kOutput, calls=%fused_computation.65 | convolution fusion | flops 48754688 | bytes 32784440 | tf_op jit(solution)/shard_map/kic,kjc->ijc/dot_general | solution.py:137
  (231 shorter events, 276.2 us)
Async XLA Ops:
  0.0 10.6 %copy-start = (bf16[32,128,128]{2,1,0:T(8,128)(2,1)S(1)}, bf16[32,128,128]{2,1,0:T(8,128)(2,1)}, u32[]{:S(2)}) copy-start(bf16[32,128,128]{2,1,0:T(8,128)(2,1)} %param.8) | copy-start | bytes 3145732
  0.0 10.6 %copy-start.20 = (f32[2,2,128]{2,1,0:T(2,128)S(1)}, f32[2,2,128]{2,1,0:T(2,128)}, u32[]{:S(2)}) copy-start(f32[2,2,128]{2,1,0:T(2,128)} %param.11) | copy-start | bytes 6148
  0.0 10.6 %copy-start.19 = (f32[2,2,128]{2,1,0:T(2,128)S(1)}, f32[2,2,128]{2,1,0:T(2,128)}, u32[]{:S(2)}) copy-start(f32[2,2,128]{2,1,0:T(2,128)} %param.12) | copy-start | bytes 6148
  6.6 5.3 copy-start.16
  15.2 10.8 %copy-start.21 = (bf16[2,128,128]{2,1,0:T(8,128)(2,1)S(1)}, bf16[2,128,128]{2,1,0:T(8,128)(2,1)}, u32[]{:S(2)}) copy-start(bf16[2,128,128]{2,1,0:T(8,128)(2,1)} %param.14) | copy-start | bytes 196612
  15.2 4.5 collective-permute-start
  15.2 27.4 %collective-permute-start.1 = (bf16[32,128,128]{2,1,0:T(8,128)(2,1)S(1)}, bf16[32,128,128]{2,1,0:T(8,128)(2,1)}, u32[]{:S(2)}, u32[]{:S(2)}) collective-permute-start(bf16[32,128,128]{2,1,0:T(8,128)(2,1)S(1)} %get-tuple-element.7), channel_id=1, source_target_pairs={{0,1},{1,0},{2,3},{3,2},{4,5},{5,4},{6,7},{7,6},{8,9},{9,8},{10,11... | collective-permute-start | bytes 3145736 | tf_op jit(solution)/shard_map/ppermute | solution.py:19
  22.6 38.8 %collective-permute-start.5 = (bf16[16,256,128]{2,1,0:T(8,128)(2,1)}, bf16[16,256,128]{2,1,0:T(8,128)(2,1)}, u32[]{:S(2)}, u32[]{:S(2)}) collective-permute-start(bf16[16,256,128]{2,1,0:T(8,128)(2,1)} %fusion.43), channel_id=1, source_target_pairs={{0,8},{2,10},{4,12},{6,14},{8,16},{10,18},{12,20},{14,22},{16,24},... | collective-permute-start | bytes 3145736 | tf_op jit(solution)/shard_map/ppermute | solution.py:25
  28.0 48.7 %collective-permute-start.4 = (bf16[16,256,128]{2,1,0:T(8,128)(2,1)}, bf16[16,256,128]{2,1,0:T(8,128)(2,1)}, u32[]{:S(2)}, u32[]{:S(2)}) collective-permute-start(bf16[16,256,128]{2,1,0:T(8,128)(2,1)} %fusion.43), channel_id=1, source_target_pairs={{0,6},{2,8},{4,10},{6,12},{8,14},{10,16},{12,18},{14,20},{16,22},{... | collective-permute-start | bytes 3145736 | tf_op jit(solution)/shard_map/ppermute | solution.py:25
  34.0 93.6 %collective-permute-start.3 = (bf16[16,256,128]{2,1,0:T(8,128)(2,1)}, bf16[16,256,128]{2,1,0:T(8,128)(2,1)}, u32[]{:S(2)}, u32[]{:S(2)}) collective-permute-start(bf16[16,256,128]{2,1,0:T(8,128)(2,1)} %fusion.43), channel_id=1, source_target_pairs={{0,4},{2,6},{4,8},{6,10},{8,12},{10,14},{12,16},{14,18},{16,20},{1... | collective-permute-start | bytes 3145736 | tf_op jit(solution)/shard_map/ppermute | solution.py:25
  36.7 111.9 %collective-permute-start.2 = (bf16[16,256,128]{2,1,0:T(8,128)(2,1)}, bf16[16,256,128]{2,1,0:T(8,128)(2,1)}, u32[]{:S(2)}, u32[]{:S(2)}) collective-permute-start(bf16[16,256,128]{2,1,0:T(8,128)(2,1)} %fusion.43), channel_id=1, source_target_pairs={{0,2},{2,4},{4,6},{6,8},{8,10},{10,12},{12,14},{14,16},{16,18},{18... | collective-permute-start | bytes 3145736 | tf_op jit(solution)/shard_map/ppermute | solution.py:25
  42.6 163.6 %collective-permute-start.6 = (bf16[16,256,128]{2,1,0:T(8,128)(2,1)}, bf16[16,256,128]{2,1,0:T(8,128)(2,1)}, u32[]{:S(2)}, u32[]{:S(2)}) collective-permute-start(bf16[16,256,128]{2,1,0:T(8,128)(2,1)} %fusion.43), channel_id=1, source_target_pairs={{0,10},{2,12},{4,14},{6,16},{8,18},{10,20},{12,22},{14,24},{16,26}... | collective-permute-start | bytes 3145736 | tf_op jit(solution)/shard_map/ppermute | solution.py:25
  61.3 152.3 %collective-permute-start.7 = (bf16[16,256,128]{2,1,0:T(8,128)(2,1)}, bf16[16,256,128]{2,1,0:T(8,128)(2,1)}, u32[]{:S(2)}, u32[]{:S(2)}) collective-permute-start(bf16[16,256,128]{2,1,0:T(8,128)(2,1)} %fusion.43), channel_id=1, source_target_pairs={{0,12},{2,14},{4,16},{6,18},{8,20},{10,22},{12,24},{14,26},{16,28}... | collective-permute-start | bytes 3145736 | tf_op jit(solution)/shard_map/ppermute | solution.py:25
  76.8 144.3 %collective-permute-start.8 = (bf16[16,256,128]{2,1,0:T(8,128)(2,1)}, bf16[16,256,128]{2,1,0:T(8,128)(2,1)}, u32[]{:S(2)}, u32[]{:S(2)}) collective-permute-start(bf16[16,256,128]{2,1,0:T(8,128)(2,1)} %fusion.43), channel_id=1, source_target_pairs={{0,14},{2,16},{4,18},{6,20},{8,22},{10,24},{12,26},{14,28},{16,30}... | collective-permute-start | bytes 3145736 | tf_op jit(solution)/shard_map/ppermute | solution.py:25
  127.6 129.7 %collective-permute-start.9 = (bf16[16,256,128]{2,1,0:T(8,128)(2,1)}, bf16[16,256,128]{2,1,0:T(8,128)(2,1)}, u32[]{:S(2)}, u32[]{:S(2)}) collective-permute-start(bf16[16,256,128]{2,1,0:T(8,128)(2,1)} %fusion.43), channel_id=1, source_target_pairs={{2,0},{4,2},{6,4},{8,6},{10,8},{12,10},{14,12},{16,14},{18,16},{20... | collective-permute-start | bytes 3145736 | tf_op jit(solution)/shard_map/ppermute | solution.py:25
  148.6 116.1 %collective-permute-start.10 = (bf16[16,256,128]{2,1,0:T(8,128)(2,1)}, bf16[16,256,128]{2,1,0:T(8,128)(2,1)}, u32[]{:S(2)}, u32[]{:S(2)}) collective-permute-start(bf16[16,256,128]{2,1,0:T(8,128)(2,1)} %fusion.43), channel_id=1, source_target_pairs={{4,0},{6,2},{8,4},{10,6},{12,8},{14,10},{16,12},{18,14},{20,16},{2... | collective-permute-start | bytes 3145736 | tf_op jit(solution)/shard_map/ppermute | solution.py:25
  206.2 103.2 %collective-permute-start.11 = (bf16[16,256,128]{2,1,0:T(8,128)(2,1)}, bf16[16,256,128]{2,1,0:T(8,128)(2,1)}, u32[]{:S(2)}, u32[]{:S(2)}) collective-permute-start(bf16[16,256,128]{2,1,0:T(8,128)(2,1)} %fusion.43), channel_id=1, source_target_pairs={{6,0},{8,2},{10,4},{12,6},{14,8},{16,10},{18,12},{20,14},{22,16},{... | collective-permute-start | bytes 3145736 | tf_op jit(solution)/shard_map/ppermute | solution.py:25
  213.6 124.2 %collective-permute-start.12 = (bf16[16,256,128]{2,1,0:T(8,128)(2,1)}, bf16[16,256,128]{2,1,0:T(8,128)(2,1)}, u32[]{:S(2)}, u32[]{:S(2)}) collective-permute-start(bf16[16,256,128]{2,1,0:T(8,128)(2,1)} %fusion.43), channel_id=1, source_target_pairs={{8,0},{10,2},{12,4},{14,6},{16,8},{18,10},{20,12},{22,14},{24,16},... | collective-permute-start | bytes 3145736 | tf_op jit(solution)/shard_map/ppermute | solution.py:25
  221.1 124.7 %collective-permute-start.13 = (bf16[16,256,128]{2,1,0:T(8,128)(2,1)}, bf16[16,256,128]{2,1,0:T(8,128)(2,1)}, u32[]{:S(2)}, u32[]{:S(2)}) collective-permute-start(bf16[16,256,128]{2,1,0:T(8,128)(2,1)} %fusion.43), channel_id=1, source_target_pairs={{10,0},{12,2},{14,4},{16,6},{18,8},{20,10},{22,12},{24,14},{26,16}... | collective-permute-start | bytes 3145736 | tf_op jit(solution)/shard_map/ppermute | solution.py:25
  257.3 96.4 %collective-permute-start.14 = (bf16[16,256,128]{2,1,0:T(8,128)(2,1)}, bf16[16,256,128]{2,1,0:T(8,128)(2,1)}, u32[]{:S(2)}, u32[]{:S(2)}) collective-permute-start(bf16[16,256,128]{2,1,0:T(8,128)(2,1)} %fusion.43), channel_id=1, source_target_pairs={{12,0},{14,2},{16,4},{18,6},{20,8},{22,10},{24,12},{26,14},{28,16}... | collective-permute-start | bytes 3145736 | tf_op jit(solution)/shard_map/ppermute | solution.py:25
  264.7 96.9 %collective-permute-start.15 = (bf16[16,256,128]{2,1,0:T(8,128)(2,1)}, bf16[16,256,128]{2,1,0:T(8,128)(2,1)}, u32[]{:S(2)}, u32[]{:S(2)}) collective-permute-start(bf16[16,256,128]{2,1,0:T(8,128)(2,1)} %fusion.43), channel_id=1, source_target_pairs={{14,0},{16,2},{18,4},{20,6},{22,8},{24,10},{26,12},{28,14},{30,16}... | collective-permute-start | bytes 3145736 | tf_op jit(solution)/shard_map/ppermute | solution.py:25
  367.3 3.6 copy-start.13
  367.3 5.4 copy-start.10
  367.3 8.9 copy-start.11
  369.1 8.9 copy-start.9
  370.9 8.9 copy-start.8
  372.7 8.9 copy-start.7
  374.5 8.9 copy-start.6
  376.2 8.8 copy-start.5
  378.0 8.8 copy-start.12
  379.8 8.7 copy-start.14
  381.5 8.7 copy-start.15
  398.4 3.3 copy-start.2
  398.5 3.3 copy-start.18
  408.7 272.1 %copy-start.22 = (bf16[2,128,128]{2,1,0:T(8,128)(2,1)S(1)}, bf16[2,128,128]{2,1,0:T(8,128)(2,1)}, u32[]{:S(2)}) copy-start(bf16[2,128,128]{2,1,0:T(8,128)(2,1)} %param.14) | copy-start | bytes 196612
  408.8 10.5 %collective-permute-start.16 = (bf16[32,128,128]{2,1,0:T(8,128)(2,1)S(1)}, bf16[32,128,128]{2,1,0:T(8,128)(2,1)S(1)}, u32[]{:S(2)}, u32[]{:S(2)}) collective-permute-start(bf16[32,128,128]{2,1,0:T(8,128)(2,1)S(1)} %get-tuple-element.6), channel_id=1, source_target_pairs={{0,1},{1,0},{2,3},{3,2},{4,5},{5,4},{6,7},{7,6},{8,9},{9,8},{10,11... | collective-permute-start | bytes 3145736 | tf_op jit(solution)/shard_map/ppermute | solution.py:19
  408.8 54.4 %collective-permute-start.17 = (bf16[32,128,128]{2,1,0:T(8,128)(2,1)}, bf16[32,128,128]{2,1,0:T(8,128)(2,1)}, u32[]{:S(2)}, u32[]{:S(2)}) collective-permute-start(bf16[32,128,128]{2,1,0:T(8,128)(2,1)} %get-tuple-element.5), channel_id=1, source_target_pairs={{0,2},{2,4},{4,6},{6,8},{8,10},{10,12},{12,14},{14,16},{16,18},{18... | collective-permute-start | bytes 3145736 | tf_op jit(solution)/shard_map/ppermute | solution.py:25
  410.8 110.8 %collective-permute-start.19 = (bf16[32,128,128]{2,1,0:T(8,128)(2,1)}, bf16[32,128,128]{2,1,0:T(8,128)(2,1)}, u32[]{:S(2)}, u32[]{:S(2)}) collective-permute-start(bf16[32,128,128]{2,1,0:T(8,128)(2,1)} %get-tuple-element.5), channel_id=1, source_target_pairs={{0,4},{2,6},{4,8},{6,10},{8,12},{10,14},{12,16},{14,18},{16,20},{1... | collective-permute-start | bytes 3145736 | tf_op jit(solution)/shard_map/ppermute | solution.py:25
  412.9 110.6 %collective-permute-start.21 = (bf16[32,128,128]{2,1,0:T(8,128)(2,1)}, bf16[32,128,128]{2,1,0:T(8,128)(2,1)}, u32[]{:S(2)}, u32[]{:S(2)}) collective-permute-start(bf16[32,128,128]{2,1,0:T(8,128)(2,1)} %get-tuple-element.5), channel_id=1, source_target_pairs={{0,6},{2,8},{4,10},{6,12},{8,14},{10,16},{12,18},{14,20},{16,22},{... | collective-permute-start | bytes 3145736 | tf_op jit(solution)/shard_map/ppermute | solution.py:25
  414.8 112.1 %collective-permute-start.23 = (bf16[32,128,128]{2,1,0:T(8,128)(2,1)}, bf16[32,128,128]{2,1,0:T(8,128)(2,1)}, u32[]{:S(2)}, u32[]{:S(2)}) collective-permute-start(bf16[32,128,128]{2,1,0:T(8,128)(2,1)} %get-tuple-element.5), channel_id=1, source_target_pairs={{0,8},{2,10},{4,12},{6,14},{8,16},{10,18},{12,20},{14,22},{16,24},... | collective-permute-start | bytes 3145736 | tf_op jit(solution)/shard_map/ppermute | solution.py:25
  420.2 203.4 %collective-permute-start.25 = (bf16[32,128,128]{2,1,0:T(8,128)(2,1)}, bf16[32,128,128]{2,1,0:T(8,128)(2,1)}, u32[]{:S(2)}, u32[]{:S(2)}) collective-permute-start(bf16[32,128,128]{2,1,0:T(8,128)(2,1)} %get-tuple-element.5), channel_id=1, source_target_pairs={{0,10},{2,12},{4,14},{6,16},{8,18},{10,20},{12,22},{14,24},{16,26}... | collective-permute-start | bytes 3145736 | tf_op jit(solution)/shard_map/ppermute | solution.py:25
  463.2 162.5 %collective-permute-start.27 = (bf16[32,128,128]{2,1,0:T(8,128)(2,1)}, bf16[32,128,128]{2,1,0:T(8,128)(2,1)}, u32[]{:S(2)}, u32[]{:S(2)}) collective-permute-start(bf16[32,128,128]{2,1,0:T(8,128)(2,1)} %get-tuple-element.5), channel_id=1, source_target_pairs={{0,12},{2,14},{4,16},{6,18},{8,20},{10,22},{12,24},{14,26},{16,28}... | collective-permute-start | bytes 3145736 | tf_op jit(solution)/shard_map/ppermute | solution.py:25
  521.6 106.0 %collective-permute-start.29 = (bf16[32,128,128]{2,1,0:T(8,128)(2,1)}, bf16[32,128,128]{2,1,0:T(8,128)(2,1)}, u32[]{:S(2)}, u32[]{:S(2)}) collective-permute-start(bf16[32,128,128]{2,1,0:T(8,128)(2,1)} %get-tuple-element.5), channel_id=1, source_target_pairs={{0,14},{2,16},{4,18},{6,20},{8,22},{10,24},{12,26},{14,28},{16,30}... | collective-permute-start | bytes 3145736 | tf_op jit(solution)/shard_map/ppermute | solution.py:25
  523.5 146.3 %collective-permute-start.31 = (bf16[32,128,128]{2,1,0:T(8,128)(2,1)}, bf16[32,128,128]{2,1,0:T(8,128)(2,1)}, u32[]{:S(2)}, u32[]{:S(2)}) collective-permute-start(bf16[32,128,128]{2,1,0:T(8,128)(2,1)} %get-tuple-element.5), channel_id=1, source_target_pairs={{2,0},{4,2},{6,4},{8,6},{10,8},{12,10},{14,12},{16,14},{18,16},{20... | collective-permute-start | bytes 3145736 | tf_op jit(solution)/shard_map/ppermute | solution.py:25
  526.9 148.8 %collective-permute-start.33 = (bf16[32,128,128]{2,1,0:T(8,128)(2,1)}, bf16[32,128,128]{2,1,0:T(8,128)(2,1)}, u32[]{:S(2)}, u32[]{:S(2)}) collective-permute-start(bf16[32,128,128]{2,1,0:T(8,128)(2,1)} %get-tuple-element.5), channel_id=1, source_target_pairs={{4,0},{6,2},{8,4},{10,6},{12,8},{14,10},{16,12},{18,14},{20,16},{2... | collective-permute-start | bytes 3145736 | tf_op jit(solution)/shard_map/ppermute | solution.py:25
  623.7 103.8 %collective-permute-start.35 = (bf16[32,128,128]{2,1,0:T(8,128)(2,1)}, bf16[32,128,128]{2,1,0:T(8,128)(2,1)}, u32[]{:S(2)}, u32[]{:S(2)}) collective-permute-start(bf16[32,128,128]{2,1,0:T(8,128)(2,1)} %get-tuple-element.5), channel_id=1, source_target_pairs={{6,0},{8,2},{10,4},{12,6},{14,8},{16,10},{18,12},{20,14},{22,16},{... | collective-permute-start | bytes 3145736 | tf_op jit(solution)/shard_map/ppermute | solution.py:25
  625.6 106.5 %collective-permute-start.37 = (bf16[32,128,128]{2,1,0:T(8,128)(2,1)}, bf16[32,128,128]{2,1,0:T(8,128)(2,1)}, u32[]{:S(2)}, u32[]{:S(2)}) collective-permute-start(bf16[32,128,128]{2,1,0:T(8,128)(2,1)} %get-tuple-element.5), channel_id=1, source_target_pairs={{8,0},{10,2},{12,4},{14,6},{16,8},{18,10},{20,12},{22,14},{24,16},... | collective-permute-start | bytes 3145736 | tf_op jit(solution)/shard_map/ppermute | solution.py:25
  627.6 109.1 %collective-permute-start.39 = (bf16[32,128,128]{2,1,0:T(8,128)(2,1)}, bf16[32,128,128]{2,1,0:T(8,128)(2,1)}, u32[]{:S(2)}, u32[]{:S(2)}) collective-permute-start(bf16[32,128,128]{2,1,0:T(8,128)(2,1)} %get-tuple-element.5), channel_id=1, source_target_pairs={{10,0},{12,2},{14,4},{16,6},{18,8},{20,10},{22,12},{24,14},{26,16}... | collective-permute-start | bytes 3145736 | tf_op jit(solution)/shard_map/ppermute | solution.py:25
  669.8 83.2 %collective-permute-start.41 = (bf16[32,128,128]{2,1,0:T(8,128)(2,1)}, bf16[32,128,128]{2,1,0:T(8,128)(2,1)}, u32[]{:S(2)}, u32[]{:S(2)}) collective-permute-start(bf16[32,128,128]{2,1,0:T(8,128)(2,1)} %get-tuple-element.5), channel_id=1, source_target_pairs={{12,0},{14,2},{16,4},{18,6},{20,8},{22,10},{24,12},{26,14},{28,16}... | collective-permute-start | bytes 3145736 | tf_op jit(solution)/shard_map/ppermute | solution.py:25
  675.7 100.2 %collective-permute-start.43 = (bf16[32,128,128]{2,1,0:T(8,128)(2,1)}, bf16[32,128,128]{2,1,0:T(8,128)(2,1)}, u32[]{:S(2)}, u32[]{:S(2)}) collective-permute-start(bf16[32,128,128]{2,1,0:T(8,128)(2,1)} %get-tuple-element.5), channel_id=1, source_target_pairs={{14,0},{16,2},{18,4},{20,6},{22,8},{24,10},{26,12},{28,14},{30,16}... | collective-permute-start | bytes 3145736 | tf_op jit(solution)/shard_map/ppermute | solution.py:25
  727.5 54.9 %collective-permute-start.18 = (bf16[32,32,128]{2,1,0:T(8,128)(2,1)}, bf16[32,32,128]{2,1,0:T(8,128)(2,1)}, u32[]{:S(2)}, u32[]{:S(2)}) collective-permute-start(bf16[32,32,128]{2,1,0:T(8,128)(2,1)} %bitcast.54), channel_id=1, source_target_pairs={{0,2},{2,4},{4,6},{6,8},{8,10},{10,12},{12,14},{14,16},{16,18},{18... | collective-permute-start | bytes 786440 | tf_op jit(solution)/shard_map/ppermute | solution.py:25
  732.1 59.3 %collective-permute-start.20 = (bf16[32,32,128]{2,1,0:T(8,128)(2,1)}, bf16[32,32,128]{2,1,0:T(8,128)(2,1)}, u32[]{:S(2)}, u32[]{:S(2)}) collective-permute-start(bf16[32,32,128]{2,1,0:T(8,128)(2,1)} %bitcast.55), channel_id=1, source_target_pairs={{0,4},{2,6},{4,8},{6,10},{8,12},{10,14},{12,16},{14,18},{16,20},{1... | collective-permute-start | bytes 786440 | tf_op jit(solution)/shard_map/ppermute | solution.py:25
  736.7 63.5 %collective-permute-start.22 = (bf16[32,32,128]{2,1,0:T(8,128)(2,1)}, bf16[32,32,128]{2,1,0:T(8,128)(2,1)}, u32[]{:S(2)}, u32[]{:S(2)}) collective-permute-start(bf16[32,32,128]{2,1,0:T(8,128)(2,1)} %bitcast.56), channel_id=1, source_target_pairs={{0,6},{2,8},{4,10},{6,12},{8,14},{10,16},{12,18},{14,20},{16,22},{... | collective-permute-start | bytes 786440 | tf_op jit(solution)/shard_map/ppermute | solution.py:25
  753.0 65.6 %collective-permute-start.24 = (bf16[32,32,128]{2,1,0:T(8,128)(2,1)}, bf16[32,32,128]{2,1,0:T(8,128)(2,1)}, u32[]{:S(2)}, u32[]{:S(2)}) collective-permute-start(bf16[32,32,128]{2,1,0:T(8,128)(2,1)} %bitcast.57), channel_id=1, source_target_pairs={{0,8},{2,10},{4,12},{6,14},{8,16},{10,18},{12,20},{14,22},{16,24},... | collective-permute-start | bytes 786440 | tf_op jit(solution)/shard_map/ppermute | solution.py:25
  775.9 54.2 %collective-permute-start.26 = (bf16[32,32,128]{2,1,0:T(8,128)(2,1)}, bf16[32,32,128]{2,1,0:T(8,128)(2,1)S(1)}, u32[]{:S(2)}, u32[]{:S(2)}) collective-permute-start(bf16[32,32,128]{2,1,0:T(8,128)(2,1)} %bitcast.58), channel_id=1, source_target_pairs={{0,10},{2,12},{4,14},{6,16},{8,18},{10,20},{12,22},{14,24},{16,26}... | collective-permute-start | bytes 786440 | tf_op jit(solution)/shard_map/ppermute | solution.py:25
  782.4 56.7 %collective-permute-start.28 = (bf16[32,32,128]{2,1,0:T(8,128)(2,1)}, bf16[32,32,128]{2,1,0:T(8,128)(2,1)}, u32[]{:S(2)}, u32[]{:S(2)}) collective-permute-start(bf16[32,32,128]{2,1,0:T(8,128)(2,1)} %bitcast.59), channel_id=1, source_target_pairs={{0,12},{2,14},{4,16},{6,18},{8,20},{10,22},{12,24},{14,26},{16,28}... | collective-permute-start | bytes 786440 | tf_op jit(solution)/shard_map/ppermute | solution.py:25
  791.3 58.5 %collective-permute-start.30 = (bf16[32,32,128]{2,1,0:T(8,128)(2,1)}, bf16[32,32,128]{2,1,0:T(8,128)(2,1)}, u32[]{:S(2)}, u32[]{:S(2)}) collective-permute-start(bf16[32,32,128]{2,1,0:T(8,128)(2,1)} %bitcast.60), channel_id=1, source_target_pairs={{0,14},{2,16},{4,18},{6,20},{8,22},{10,24},{12,26},{14,28},{16,30}... | collective-permute-start | bytes 786440 | tf_op jit(solution)/shard_map/ppermute | solution.py:25
  800.2 63.1 %collective-permute-start.32 = (bf16[32,32,128]{2,1,0:T(8,128)(2,1)}, bf16[32,32,128]{2,1,0:T(8,128)(2,1)}, u32[]{:S(2)}, u32[]{:S(2)}) collective-permute-start(bf16[32,32,128]{2,1,0:T(8,128)(2,1)} %bitcast.61), channel_id=1, source_target_pairs={{2,0},{4,2},{6,4},{8,6},{10,8},{12,10},{14,12},{16,14},{18,16},{20... | collective-permute-start | bytes 786440 | tf_op jit(solution)/shard_map/ppermute | solution.py:25
  818.5 61.6 %collective-permute-start.34 = (bf16[32,32,128]{2,1,0:T(8,128)(2,1)}, bf16[32,32,128]{2,1,0:T(8,128)(2,1)}, u32[]{:S(2)}, u32[]{:S(2)}) collective-permute-start(bf16[32,32,128]{2,1,0:T(8,128)(2,1)} %bitcast.62), channel_id=1, source_target_pairs={{4,0},{6,2},{8,4},{10,6},{12,8},{14,10},{16,12},{18,14},{20,16},{2... | collective-permute-start | bytes 786440 | tf_op jit(solution)/shard_map/ppermute | solution.py:25
  830.0 64.8 %collective-permute-start.36 = (bf16[32,32,128]{2,1,0:T(8,128)(2,1)}, bf16[32,32,128]{2,1,0:T(8,128)(2,1)}, u32[]{:S(2)}, u32[]{:S(2)}) collective-permute-start(bf16[32,32,128]{2,1,0:T(8,128)(2,1)} %bitcast.63), channel_id=1, source_target_pairs={{6,0},{8,2},{10,4},{12,6},{14,8},{16,10},{18,12},{20,14},{22,16},{... | collective-permute-start | bytes 786440 | tf_op jit(solution)/shard_map/ppermute | solution.py:25
  839.1 62.6 %collective-permute-start.38 = (bf16[32,32,128]{2,1,0:T(8,128)(2,1)}, bf16[32,32,128]{2,1,0:T(8,128)(2,1)S(1)}, u32[]{:S(2)}, u32[]{:S(2)}) collective-permute-start(bf16[32,32,128]{2,1,0:T(8,128)(2,1)} %bitcast.64), channel_id=1, source_target_pairs={{8,0},{10,2},{12,4},{14,6},{16,8},{18,10},{20,12},{22,14},{24,16},... | collective-permute-start | bytes 786440 | tf_op jit(solution)/shard_map/ppermute | solution.py:25
  849.8 57.8 %collective-permute-start.40 = (bf16[32,32,128]{2,1,0:T(8,128)(2,1)}, bf16[32,32,128]{2,1,0:T(8,128)(2,1)}, u32[]{:S(2)}, u32[]{:S(2)}) collective-permute-start(bf16[32,32,128]{2,1,0:T(8,128)(2,1)} %bitcast.65), channel_id=1, source_target_pairs={{10,0},{12,2},{14,4},{16,6},{18,8},{20,10},{22,12},{24,14},{26,16}... | collective-permute-start | bytes 786440 | tf_op jit(solution)/shard_map/ppermute | solution.py:25
  863.2 51.3 %collective-permute-start.42 = (bf16[32,32,128]{2,1,0:T(8,128)(2,1)}, bf16[32,32,128]{2,1,0:T(8,128)(2,1)}, u32[]{:S(2)}, u32[]{:S(2)}) collective-permute-start(bf16[32,32,128]{2,1,0:T(8,128)(2,1)} %bitcast.66), channel_id=1, source_target_pairs={{12,0},{14,2},{16,4},{18,6},{20,8},{22,10},{24,12},{26,14},{28,16}... | collective-permute-start | bytes 786440 | tf_op jit(solution)/shard_map/ppermute | solution.py:25
  880.1 41.3 %collective-permute-start.44 = (bf16[32,32,128]{2,1,0:T(8,128)(2,1)}, bf16[32,32,128]{2,1,0:T(8,128)(2,1)}, u32[]{:S(2)}, u32[]{:S(2)}) collective-permute-start(bf16[32,32,128]{2,1,0:T(8,128)(2,1)} %bitcast.67), channel_id=1, source_target_pairs={{14,0},{16,2},{18,4},{20,6},{22,8},{24,10},{26,12},{28,14},{30,16}... | collective-permute-start | bytes 786440 | tf_op jit(solution)/shard_map/ppermute | solution.py:25
  (5 other events, 9.9 us)
where the time goes:
time: 954 us; the launch traced here: 941 us
  starting transfers between devices  326 us (34%)
  waiting for transfers between devices  254 us (27%)
  local copies, waits for them, and re-layouts  191 us (20%)
  matrix products  109 us (11%)
  other arithmetic  54.3 us (6%)
    ppermute x42, starting transfers between devices, shifted(): return lax.ppermute(value, axis, pairs)  326 us
    ppermute x42, waiting for transfers between devices, shifted(): return lax.ppermute(value, axis, pairs)  252 us
    ppermute x42, local copies, waits for them, and re-layouts, shifted(): return lax.ppermute(value, axis, pairs)  122 us
    dot_general x14, matrix products, body(): jnp.einsum('kic,kjc->ijc', got_left, got_right, preferred_element_type=jn...  54.6 us
    dot_general x15, matrix products, body(): jnp.einsum('ikc,ukc->iuc', left_full, segment, preferred_element_type=jnp...  43.2 us
    dot_general x15, local copies, waits for them, and re-layouts, body(): jnp.einsum('ikc,ukc->iuc', left_full, segment, preferred_element_type=jnp...  33.5 us
    dynamic_update_slice x15, other arithmetic, body(): lax.dynamic_update_slice_in_dim(summed, current + usable * product[:, Non...  25.3 us
  transfers between devices with their start and end apart: 45, of which 10 were waited for; matrix products, arithmetic and copies ran while one was open for 29% of the time, Pallas kernels for 0%

commit v1 on v0

v1 whole, which is shorter than its diff:
```python
import functools

import jax
import jax.numpy as jnp
from jax import lax
from jax.experimental import pallas as pl
from jax.experimental.pallas import tpu as pltpu
from jax.sharding import PartitionSpec as P

EPS = 1e-05
CH = 128
ROWS = 32
HALF = 16
SPAN = 8
COMPLEXES = 16
DEV_ROWS = 64
DEVS = 128
F32 = jnp.float32
BF16 = jnp.bfloat16
MESH = pl.DeviceIdType.MESH


def sigmoid(x):
    return 0.5 * jnp.tanh(0.5 * x) + 0.5


def flip(x):
    eye = (
        lax.broadcasted_iota(jnp.int32, (CH, CH), 0) == lax.broadcasted_iota(jnp.int32, (CH, CH), 1)
    ).astype(F32).astype(BF16)
    return lax.dot_general(eye, x, (((1,), (1,)), ((), ())), preferred_element_type=F32)


def norm(x, gain, bias):
    average = jnp.sum(x, axis=0, keepdims=True) * (1.0 / CH)
    centred = x - average
    variance = jnp.sum(centred * centred, axis=0, keepdims=True) * (1.0 / CH)
    return (centred * lax.rsqrt(variance + EPS) * gain + bias).astype(BF16)


def prepare(gain_ref, bias_ref, proj_ref, gate_ref, out_ref, wt, wo, gb):
    for layer in range(2):
        for blk in range(4):
            part = slice(blk * CH, (blk + 1) * CH)
            wt[layer, part] = flip(proj_ref[layer, :, part]).astype(BF16)
        wt[layer, 4 * CH :] = flip(gate_ref[layer]).astype(BF16)
        wo[layer] = flip(out_ref[layer]).astype(BF16)
        for which in range(2):
            for kind, ref in enumerate((gain_ref, bias_ref)):
                line = ref[layer, pl.ds(which, 1), :]
                gb[layer, which, kind] = jnp.transpose(jnp.broadcast_to(line, (CH, CH)))


def project(layer, pair, i, inside, wt, gb, gating, fact):
    gain, bias = gb[layer, 0, 0], gb[layer, 0, 1]
    zn = jnp.concatenate([norm(z, gain, bias) for z in pair], axis=1)
    p = jnp.dot(wt[layer], zn, preferred_element_type=F32)
    for e in range(2):
        q = p[:, e * CH : (e + 1) * CH]
        left = jnp.where(inside, sigmoid(q[:CH]) * q[CH : 2 * CH], 0.0)
        right = jnp.where(inside, sigmoid(q[2 * CH : 3 * CH]) * q[3 * CH : 4 * CH], 0.0)
        fact[0, pl.ds(i + e, CH, stride=HALF), :] = left
        fact[1, pl.ds(i + e, CH, stride=HALF), :] = right
        gating[e] = sigmoid(q[4 * CH :])


def pack(fact, send):
    def step(t, carry):
        for f in range(2):
            block = fact[f, pl.ds(pl.multiple_of(t * 256, 256), 256), :]
            send[pl.ds(t * 16, 16), f] = block.reshape(16, HALF, CH).astype(BF16)
        return carry

    lax.fori_loop(0, 8, step, 0)


def first_half(half, z_ref, inside, wt, gb, zt, gating, fact, send):
    def step(t, carry):
        i = 2 * t
        row = half * HALF + i
        pair = [flip(z_ref[row + e]) for e in range(2)]
        for e in range(2):
            zt[row + e] = pair[e].astype(BF16)
        project(0, pair, i, inside, wt, gb, gating.at[pl.ds(row, 2)], fact)
        return carry

    lax.fori_loop(0, HALF // 2, step, 0)
    pack(fact, send)


def updated(layer, row, i, inside, wo, gb, zt, gating, sums):
    gain, bias = gb[layer, 1, 0], gb[layer, 1, 1]
    normed = jnp.concatenate(
        [norm(sums[pl.ds(i + e, CH, stride=HALF), :], gain, bias) for e in range(2)], axis=1
    )
    u = jnp.dot(wo[layer], normed, preferred_element_type=F32)
    return [
        jnp.where(
            inside, zt[row + e].astype(F32) + gating[row + e] * u[:, e * CH : (e + 1) * CH], 0.0
        ).astype(BF16)
        for e in range(2)
    ]


def unpack(got, sums):
    def step(t, carry):
        block = got[pl.ds(t * 16, 16)].astype(F32)
        sums[pl.ds(pl.multiple_of(t * 256, 256), 256), :] = block.reshape(256, CH)
        return carry

    lax.fori_loop(0, 8, step, 0)


def middle_half(half, got, inside, wt, wo, gb, zt, gating, sums, fact, send):
    unpack(got, sums)

    def step(t, carry):
        i = 2 * t
        row = half * HALF + i
        pair = updated(0, row, i, inside, wo, gb, zt, gating, sums)
        for e in range(2):
            zt[row + e] = pair[e]
        project(
            1, [z.astype(F32) for z in pair], i, inside, wt, gb, gating.at[pl.ds(row, 2)], fact
        )
        return carry

    lax.fori_loop(0, HALF // 2, step, 0)
    pack(fact, send)


def last_half(half, got, inside, wo, gb, zt, gating, sums, o_ref):
    unpack(got, sums)

    def step(t, carry):
        i = 2 * t
        row = half * HALF + i
        pair = updated(1, row, i, inside, wo, gb, zt, gating, sums)
        for e in range(2):
            o_ref[row + e] = flip(pair[e]).astype(BF16)
        return carry

    lax.fori_loop(0, HALF // 2, step, 0)


def triangle(layer, begin_ref, extent_ref, recv, block_sums):
    dims = (((1,), (1,)), ((), ())) if layer == 0 else (((0,), (0,)), ((), ()))

    def step(b, carry):
        begin = begin_ref[b]
        ours = lax.broadcasted_iota(jnp.int32, (SPAN, HALF, CH), 0) < extent_ref[b]

        def window(f):
            tall = []
            for half in range(2):
                wide = [
                    jnp.where(ours, recv[pl.ds(begin, SPAN), h, half, f], jnp.zeros((), BF16)).reshape(CH, CH)
                    for h in range(2)
                ]
                tall.append(jnp.concatenate(wide, axis=1))
            return jnp.concatenate(tall, axis=0)

        s = lax.dot_general(window(0), window(1), dims, preferred_element_type=F32).astype(BF16)
        for hi in range(2):
            for hj in range(2):
                block_sums[b, hj, hi] = s[hi * CH : (hi + 1) * CH, hj * CH : (hj + 1) * CH].reshape(
                    SPAN, HALF, CH
                )
        return carry

    lax.fori_loop(0, COMPLEXES, step, 0)


def spread(member_ref, place_ref, block_sums, send, half):
    def step(r, carry):
        b, q = member_ref[r], place_ref[r]
        for hj in range(2):
            send[2 * r + hj] = block_sums[b, hj, half, q]
        return carry

    lax.fori_loop(0, DEV_ROWS, step, 0)


def inside_mask(extent):
    return lax.broadcasted_iota(jnp.int32, (1, CH), 1) < extent * HALF


def k_first(own_ref, z_ref, gain_ref, bias_ref, proj_ref, gate_ref, outw_ref, zt, gating, send, wt, wo, gb, fact):
    prepare(gain_ref, bias_ref, proj_ref, gate_ref, outw_ref, wt, wo, gb)
    inside = inside_mask(own_ref[0])
    for half in range(2):
        first_half(half, z_ref, inside, wt, gb, zt, gating, fact, send.at[half])


def k_triangle(layer, begin_ref, extent_ref, member_ref, place_ref, got, send, recv, block_sums):
    recv[pl.ds(DEV_ROWS, SPAN)] = jnp.zeros((SPAN,) + recv.shape[1:], BF16)

    def move(r, carry):
        for half in range(2):
            for h in range(2):
                recv[r, h, half] = got[half, 2 * r + h]
        return carry

    lax.fori_loop(0, DEV_ROWS, move, 0)
    triangle(layer, begin_ref, extent_ref, recv, block_sums)
    for half in range(2):
        spread(member_ref, place_ref, block_sums, send.at[half], half)


def k_middle(own_ref, got, zt_in, gating_in, wt, wo, gb, zt, gating, send, sums, fact):
    inside = inside_mask(own_ref[0])
    zt[...] = zt_in[...]
    gating[...] = gating_in[...]
    for half in range(2):
        middle_half(half, got.at[half], inside, wt, wo, gb, zt, gating, sums, fact, send.at[half])


def k_last(own_ref, got, zt, gating, wo, gb, o_ref, sums):
    inside = inside_mask(own_ref[0])
    for half in range(2):
        last_half(half, got.at[half], inside, wo, gb, zt, gating, sums, o_ref)


def body(pair_rep, token_counts, first_device, norm_gain, norm_bias, proj_weight, gate_weight, out_weight):
    row = lax.axis_index("row")
    extents = token_counts // ROWS
    rows = jnp.arange(DEV_ROWS, dtype=jnp.int32)
    member = jnp.sum((first_device[None, :] <= rows[:, None]).astype(jnp.int32), 1) - 1
    place = rows - first_device[member]
    own = extents[member[row]].reshape(1)
    smem = pl.BlockSpec(memory_space=pltpu.SMEM)
    vmem = pl.BlockSpec(memory_space=pltpu.VMEM)
    params = pltpu.CompilerParams(vmem_limit_bytes=48 * 2**20)
    S = jax.ShapeDtypeStruct
    zt_s, gating_s = S((ROWS, CH, CH), BF16), S((ROWS, CH, CH), F32)
    send_s = S((2, DEVS, 2, HALF, CH), BF16)
    back_s = S((2, DEVS, HALF, CH), BF16)
    wt_s, wo_s, gb_s = S((2, 5 * CH, CH), BF16), S((2, CH, CH), BF16), S((2, 2, 2, CH, CH), F32)
    fact_s = pltpu.VMEM((2, CH * HALF, CH), F32)
    sums_s = pltpu.VMEM((CH * HALF, CH), F32)

    def a2a(x):
        return lax.all_to_all(x, ("row", "col"), 1, 1, tiled=True)

    def tri(layer, got):
        return pl.pallas_call(
            functools.partial(k_triangle, layer),
            out_shape=back_s,
            in_specs=[smem] * 4 + [vmem],
            out_specs=vmem,
            scratch_shapes=[
                pltpu.VMEM((DEV_ROWS + SPAN, 2, 2, 2, HALF, CH), BF16),
                pltpu.VMEM((COMPLEXES, 2, 2, SPAN, HALF, CH), BF16),
            ],
            compiler_params=params,
        )(first_device, extents, member, place, got)

    zt, gating, send, wt, wo, gb = pl.pallas_call(
        k_first,
        out_shape=(zt_s, gating_s, send_s, wt_s, wo_s, gb_s),
        in_specs=[smem] + [vmem] * 6,
        out_specs=[vmem] * 6,
        scratch_shapes=[fact_s],
        compiler_params=params,
    )(own, pair_rep, norm_gain, norm_bias, proj_weight, gate_weight, out_weight)
    back = a2a(tri(0, a2a(send)))
    zt, gating, send = pl.pallas_call(
        k_middle,
        out_shape=(zt_s, gating_s, send_s),
        in_specs=[smem] + [vmem] * 6,
        out_specs=[vmem] * 3,
        scratch_shapes=[sums_s, fact_s],
        compiler_params=params,
    )(own, back, zt, gating, wt, wo, gb)
    back = a2a(tri(1, a2a(send)))
    return pl.pallas_call(
        k_last,
        out_shape=S((ROWS, CH, CH), BF16),
        in_specs=[smem] + [vmem] * 5,
        out_specs=vmem,
        scratch_shapes=[sums_s],
        compiler_params=params,
    )(own, back, zt, gating, wo, gb)


def solution(mesh):
    return jax.shard_map(
        body,
        mesh=mesh,
        in_specs=(P("row", "col", None), P(), P(), P(), P(), P(), P(), P()),
        out_specs=P("row", "col", None),
        check_vma=False,
    )
```

time: 954 us -> 189 us (0.20)
  the two profiles are of different devices: /device:TPU:16 before, /device:TPU:1 now
where the time goes in v1:
time: 189 us; the launch traced here: 188 us
  blocking collectives  81.2 us (43%)
  Pallas kernels  44.9 us (24%)
  waiting for transfers between devices  29.1 us (15%)
  local copies, waits for them, and re-layouts  17.5 us (9%)
  starting transfers between devices  12 us (6%)
  between operations  2.05 us (1%)
    all_to_all x3, blocking collectives, a2a(): return lax.all_to_all(x, ('row', 'col'), 1, 1, tiled=True)  81.2 us
    all_to_all x1, waiting for transfers between devices, a2a(): return lax.all_to_all(x, ('row', 'col'), 1, 1, tiled=True)  29.1 us
    pallas_call x1, Pallas kernels, body(): pl.pallas_call(k_middle, out_shape=(zt_s, gating_s, send_s), in_specs=[sm...  14.2 us
    all_to_all x1, starting transfers between devices, a2a(): return lax.all_to_all(x, ('row', 'col'), 1, 1, tiled=True)  12 us
    pallas_call x2, Pallas kernels, tri(): pl.pallas_call(functools.partial(k_triangle, layer), out_shape=back_s, in...  11.3 us
    pallas_call x1, Pallas kernels, body(): pl.pallas_call(k_first, out_shape=(zt_s, gating_s, send_s, wt_s, wo_s, gb...  11 us
    pallas_call x1, Pallas kernels, body(): pl.pallas_call(k_last, out_shape=S((ROWS, CH, CH), BF16), in_specs=[smem]...  8.4 us
    unnamed x16, local copies, waits for them, and re-layouts  6.56 us
  transfers between devices with their start and end apart: 1, of which 1 were waited for; matrix products, arithmetic and copies ran while one was open for 0% of the time, Pallas kernels for 0%

profile of v1, /device:TPU:1, one launch (start us, length us, event | category | flops | bytes accessed | tf_op | source)
XLA Modules:
  0.0 188.1 jit_solution(15617006857033464586)
XLA Ops:
  0.0 0.7 and_select_fusion.extent_ref
  0.7 0.7 convert_reduce_fusion
  1.4 0.6 dynamic_slice.6
  3.9 0.6 dynamic_slice.7.own_ref
  4.6 0.0 copy-start.2
  4.6 1.2 copy-done.2
  5.8 0.0 copy-start.3
  5.8 0.9 copy-done.3
  6.7 0.0 copy-start.4
  6.7 0.8 copy-done.4
  7.6 0.0 copy-start.5
  7.6 0.8 copy-done.5
  8.4 0.0 copy-start.6
  8.4 0.7 copy-done.6
  9.1 0.0 copy-start.7
  9.1 0.7 copy-done.7
  9.8 11.0 %shard_map.82 = (bf16[32,128,128]{2,1,0:T(8,128)(2,1)S(1)}, f32[32,128,128]{2,1,0:T(8,128)S(1)}, bf16[2,128,2,16,128]{4,3,2,1,0:T(8,128)(2,1)}, bf16[2,640,128]{...) custom-call(s32[1]{0:T(128)} %dynamic_slice.7.own_ref, ...), custom_call_target="tpu_custom_call" | custom-call | tf_op jit(solution)/shard_map/pallas_call | solution.py:258
  20.8 0.0 copy-start.1
  20.8 1.3 copy-done.1
  22.2 3.6 %copy.17 = bf16[2,128,2,16,128]{4,3,2,0,1:T(8,128)(2,1)} copy(bf16[2,128,2,16,128]{4,3,2,1,0:T(8,128)(2,1)} %get-tuple-element.14) | data formatting | bytes 4194304 | tf_op jit(solution)/shard_map/pallas_call | solution.py:258
  25.8 0.0 copy-start
  25.8 12.0 %all-to-all-start = ((bf16[2,128,2,16,128]{4,3,2,0,1:T(8,128)(2,1)}), bf16[2,128,2,16,128]{4,3,2,0,1:T(8,128)(2,1)}, u32[]{:S(2)}, u32[]{:S(2)}) async-start(bf16[2,128,2,16,128]{4,3,2,0,1:T(8,128)(2,1)} %copy.17), calls=%async_computation | async-start | bytes 4194304 | tf_op jit(solution)/shard_map/all_to_all | solution.py:243
  37.8 0.0 copy-done
  37.8 0.8 gather_fusion
  38.6 29.1 %all-to-all-done = bf16[2,128,2,16,128]{4,3,2,0,1:T(8,128)(2,1)} async-done(((bf16[2,128,2,16,128]{4,3,2,0,1:T(8,128)(2,1)}), bf16[2,128,2,16,128]{4,3,2,0,1:T(8,128)(2,1)}, u32[]{:S(2)}, u32[]{:S(2)}) %all-to-all-start) | async-done | bytes 2097184 | tf_op jit(solution)/shard_map/all_to_all | solution.py:243
  67.6 2.0 %copy.18.got = bf16[2,128,2,16,128]{4,3,2,1,0:T(8,128)(2,1)S(1)} copy(bf16[2,128,2,16,128]{4,3,2,0,1:T(8,128)(2,1)} %all-to-all-done) | data formatting | bytes 4194304 | tf_op jit(solution)/shard_map/all_to_all | solution.py:243
  69.6 5.6 %shard_map.83 = bf16[2,128,16,128]{3,2,1,0:T(8,128)(2,1)S(1)} custom-call(s32[16]{0:T(128)S(1)} %copy-done, s32[16]{0:T(128)S(1)} %and_select_fusion.extent_ref, s32[64]{0:T(128)S(1)} %broadcast_add_fusion.member_ref, s32[64]{0:T(128)S(1)} %iota_subtract_fusion.place_ref, bf16[2,128,2,16,128]{4,3,2,1,0:T(8,128)(2,1)S(1)} %copy.18.got), custom_call_target="tpu_custom_call" | custom-call | tf_op jit(solution)/shard_map/pallas_call | solution.py:246
  75.2 0.2 copy.19
  75.4 23.3 %all_to_all.20 = bf16[2,128,16,128]{3,2,0,1:T(8,128)(2,1)S(1)} all-to-all(bf16[2,128,16,128]{3,2,0,1:T(8,128)(2,1)S(1)} %copy.19), channel_id=1, replica_groups=mesh['row'=64,'col'=2] {'row','col'}, dimensions={1} | all-to-all | bytes 2097152 | tf_op jit(solution)/shard_map/all_to_all | solution.py:243
  98.8 0.2 copy.20.got
  99.0 14.2 %shard_map.84 = (bf16[32,128,128]{2,1,0:T(8,128)(2,1)S(1)}, f32[32,128,128]{2,1,0:T(8,128)S(1)}, bf16[2,128,2,16,128]{4,3,2,1,0:T(8,128)(2,1)}) custom-call(s32[1]{0:T(128)} %dynamic_slice.7.own_ref, bf16[2,128,16,128]{3,2,1,0:T(8,128)(2,1)S(1)} %copy.20.got, bf16[32,128,128]{2,1,0:T(8,128)(2,1)S(1)} %get-tuple-element.15.zt_in, f32[32,128,128]{2,1,0:T(8,128)} %copy-done.1, ...), custom_call_target="tpu_custom_call" | custom-call | tf_op jit(solution)/shard_map/pallas_call | solution.py:267
  113.2 2.3 %copy.21 = bf16[2,128,2,16,128]{4,3,2,0,1:T(8,128)(2,1)S(1)} copy(bf16[2,128,2,16,128]{4,3,2,1,0:T(8,128)(2,1)} %get-tuple-element.20) | data formatting | bytes 4194304 | tf_op jit(solution)/shard_map/pallas_call | solution.py:267
  115.5 34.5 %all_to_all.21 = bf16[2,128,2,16,128]{4,3,2,0,1:T(8,128)(2,1)S(1)} all-to-all(bf16[2,128,2,16,128]{4,3,2,0,1:T(8,128)(2,1)S(1)} %copy.21), channel_id=1, replica_groups=mesh['row'=64,'col'=2] {'row','col'}, dimensions={1} | all-to-all | bytes 4194304 | tf_op jit(solution)/shard_map/all_to_all | solution.py:243
  149.9 0.4 copy.22.got
  150.3 5.7 %shard_map.85 = bf16[2,128,16,128]{3,2,1,0:T(8,128)(2,1)S(1)} custom-call(s32[16]{0:T(128)S(1)} %copy-done, s32[16]{0:T(128)S(1)} %and_select_fusion.extent_ref, s32[64]{0:T(128)S(1)} %broadcast_add_fusion.member_ref, s32[64]{0:T(128)S(1)} %iota_subtract_fusion.place_ref, bf16[2,128,2,16,128]{4,3,2,1,0:T(8,128)(2,1)S(1)} %copy.22.got), custom_call_target="tpu_custom_call" | custom-call | tf_op jit(solution)/shard_map/pallas_call | solution.py:246
  156.0 0.2 copy.23
  156.2 23.3 %all_to_all.22 = bf16[2,128,16,128]{3,2,0,1:T(8,128)(2,1)S(1)} all-to-all(bf16[2,128,16,128]{3,2,0,1:T(8,128)(2,1)S(1)} %copy.23), channel_id=1, replica_groups=mesh['row'=64,'col'=2] {'row','col'}, dimensions={1} | all-to-all | bytes 2097152 | tf_op jit(solution)/shard_map/all_to_all | solution.py:243
  179.5 0.2 copy.24.got
  179.7 8.4 %shard_map.86 = bf16[32,128,128]{2,1,0:T(8,128)(2,1)} custom-call(s32[1]{0:T(128)} %dynamic_slice.7.own_ref, bf16[2,128,16,128]{3,2,1,0:T(8,128)(2,1)S(1)} %copy.24.got, bf16[32,128,128]{2,1,0:T(8,128)(2,1)S(1)} %get-tuple-element.21.zt, f32[32,128,128]{2,1,0:T(8,128)S(1)} %get-tuple-element.22.gating, bf16[2,128,128]{2,1,0:T(8,128)(2,1)S(1)} %get-tuple-element.18.wo, ...), custom_call_target="tpu_custom_call" | custom-call | tf_op jit(solution)/shard_map/pallas_call | solution.py:276
  (4 shorter events, 0.0 us)
Async XLA Ops:
  4.6 1.2 copy-start.2
  5.8 0.9 copy-start.3
  6.7 0.8 copy-start.4
  7.6 0.8 copy-start.5
  8.4 0.7 copy-start.6
  9.1 0.7 copy-start.7
  20.8 1.3 copy-start.1
  25.8 12.0 %copy-start = (s32[16]{0:T(128)S(1)}, s32[16]{0:T(128)}, u32[]{:S(2)}) copy-start(s32[16]{0:T(128)} %begin_ref.3) | copy-start | bytes 196
  25.8 41.8 %all-to-all-start = ((bf16[2,128,2,16,128]{4,3,2,0,1:T(8,128)(2,1)}), bf16[2,128,2,16,128]{4,3,2,0,1:T(8,128)(2,1)}, u32[]{:S(2)}, u32[]{:S(2)}) async-start(bf16[2,128,2,16,128]{4,3,2,0,1:T(8,128)(2,1)} %copy.17), calls=%async_computation | async-start | bytes 4194304 | tf_op jit(solution)/shard_map/all_to_all | solution.py:243

commit v2 on v1

--- a/solution.py
+++ b/solution.py
@@ -143,18 +143,22 @@
     lax.fori_loop(0, HALF // 2, step, 0)
 
 
-def triangle(layer, begin_ref, extent_ref, recv, block_sums):
+def triangle(layer, begin_ref, count_ref, recv, block_sums):
     dims = (((1,), (1,)), ((), ())) if layer == 0 else (((0,), (0,)), ((), ()))
 
     def step(b, carry):
-        begin = begin_ref[b]
-        ours = lax.broadcasted_iota(jnp.int32, (SPAN, HALF, CH), 0) < extent_ref[b]
+        begin = jnp.clip(begin_ref[b], 0, DEV_ROWS - 1)
+        ours = lax.broadcasted_iota(jnp.int32, (SPAN, HALF, CH), 0) * ROWS < count_ref[b]
+
+        parts = [
+            recv[half][pl.ds(2 * begin, 2 * SPAN)].reshape(SPAN, 2, 2, HALF, CH) for half in range(2)
+        ]
 
         def window(f):
             tall = []
             for half in range(2):
                 wide = [
-                    jnp.where(ours, recv[pl.ds(begin, SPAN), h, half, f], jnp.zeros((), BF16)).reshape(CH, CH)
+                    jnp.where(ours, parts[half][:, h, f], jnp.zeros((), BF16)).reshape(CH, CH)
                     for h in range(2)
                 ]
                 tall.append(jnp.concatenate(wide, axis=1))
@@ -171,116 +175,173 @@
     lax.fori_loop(0, COMPLEXES, step, 0)
 
 
-def spread(member_ref, place_ref, block_sums, send, half):
-    def step(r, carry):
-        b, q = member_ref[r], place_ref[r]
-        for hj in range(2):
-            send[2 * r + hj] = block_sums[b, hj, half, q]
-        return carry
-
-    lax.fori_loop(0, DEV_ROWS, step, 0)
-
-
-def inside_mask(extent):
-    return lax.broadcasted_iota(jnp.int32, (1, CH), 1) < extent * HALF
-
-
-def k_first(own_ref, z_ref, gain_ref, bias_ref, proj_ref, gate_ref, outw_ref, zt, gating, send, wt, wo, gb, fact):
+def spread(begin_ref, block_sums, send):
+    def step(r, b):
+        later = jnp.minimum(b + 1, COMPLEXES - 1)
+        b = jnp.where(begin_ref[later] <= r, later, b)
+        q = jnp.clip(r - begin_ref[b], 0, SPAN - 1)
+        for half in range(2):
+            for hj in range(2):
+                send[half][2 * r + hj] = block_sums[b, hj, half, q]
+        return b
+
+    lax.fori_loop(0, DEV_ROWS, step, jnp.int32(0))
+
+
+def inside_mask(row, begin_ref, count_ref):
+    count = count_ref[0]
+    for b in range(1, COMPLEXES):
+        count = jnp.where(begin_ref[b] <= row, count_ref[b], count)
+    return lax.broadcasted_iota(jnp.int32, (1, CH), 1) * 2 < count
+
+
+def kernel(
+    count_ref, begin_ref, z_hbm, gain_hbm, bias_hbm, proj_hbm, gate_hbm, outw_hbm,
+    o_ref,
+    z_ref, gain_ref, bias_ref, proj_ref, gate_ref, outw_ref,
+    wt, wo, gb, zt, gating, fact, sums, block_sums, load_sem, send_sem, recv_sem, *exchanged,
+):
+    send, recv, back, got = [
+        [exchanged[k : k + 2], exchanged[k + 2 : k + 4]] for k in range(0, 16, 4)
+    ]
+    row, col = lax.axis_index("row"), lax.axis_index("col")
+    me = row * 2 + col
+    y, x, z = row // 16, (row // 4) % 4, row % 4
+
+    def peer(s):
+        to = ((y + s // 32) % 4) * 16 + ((x + (s // 8) % 4) % 4) * 4 + (z + (s // 2) % 4) % 4
+        return to, (col + s) % 2
+
+    loads = [
+        pltpu.make_async_copy(src, dst, load_sem.at[k])
+        for k, (src, dst) in enumerate(
+            (
+                (proj_hbm, proj_ref),
+                (gate_hbm, gate_ref),
+                (outw_hbm, outw_ref),
+                (gain_hbm, gain_ref),
+                (bias_hbm, bias_ref),
+                (z_hbm, z_ref),
+            )
+        )
+    ]
+    for load in loads:
+        load.start()
+
+    for ref in recv[0] + recv[1]:
+        ref[pl.ds(DEVS, 2 * SPAN)] = jnp.zeros((2 * SPAN,) + ref.shape[1:], BF16)
+
+    barrier = pltpu.get_barrier_semaphore()
+
+    def greet(s, carry):
+        pl.semaphore_signal(barrier, inc=1, device_id=peer(s), device_id_type=MESH)
+        return carry
+
+    lax.fori_loop(1, DEVS, greet, 0)
+
+    inside = inside_mask(row, begin_ref, count_ref)
+    for load in loads:
+        load.wait()
     prepare(gain_ref, bias_ref, proj_ref, gate_ref, outw_ref, wt, wo, gb)
-    inside = inside_mask(own_ref[0])
+
+    def deliver(src, dst, k):
+        def step(s, carry):
+            to, core = peer((s * 37) % DEVS)
+            pltpu.make_async_remote_copy(
+                src_ref=src.at[to * 2 + core],
+                dst_ref=dst.at[me],
+                send_sem=send_sem.at[k],
+                recv_sem=recv_sem.at[k],
+                device_id=(to, core),
+                device_id_type=MESH,
+            ).start()
+            return carry
+
+        lax.fori_loop(1, DEVS, step, 0)
+
+    def others(src, dst, k):
+        return pltpu.make_async_remote_copy(
+            src_ref=src.at[pl.ds(0, DEVS - 1)],
+            dst_ref=dst.at[pl.ds(0, DEVS - 1)],
+            send_sem=send_sem.at[k],
+            recv_sem=recv_sem.at[k],
+            device_id=(row, 1 - col),
+            device_id_type=MESH,
+        )
+
+    def arrived(src, dst, k):
+        others(src, dst, k).wait_recv()
+        dst[me] = src[me]
+
+    def forward(layer, half):
+        return send[layer][half], recv[layer][half], 4 * layer + half
+
+    def backward(layer, half):
+        return back[layer][half], got[layer][half], 4 * layer + 2 + half
+
+    def product(layer):
+        for half in range(2):
+            arrived(*forward(layer, half))
+        triangle(layer, begin_ref, count_ref, recv[layer], block_sums)
+        spread(begin_ref, block_sums, back[layer])
+        for half in range(2):
+            deliver(*backward(layer, half))
+
     for half in range(2):
-        first_half(half, z_ref, inside, wt, gb, zt, gating, fact, send.at[half])
-
-
-def k_triangle(layer, begin_ref, extent_ref, member_ref, place_ref, got, send, recv, block_sums):
-    recv[pl.ds(DEV_ROWS, SPAN)] = jnp.zeros((SPAN,) + recv.shape[1:], BF16)
-
-    def move(r, carry):
+        first_half(half, z_ref, inside, wt, gb, zt, gating, fact, send[0][half])
+        if half == 0:
+            pl.semaphore_wait(barrier, DEVS - 1)
+        deliver(*forward(0, half))
+    product(0)
+    for half in range(2):
+        arrived(*backward(0, half))
+        middle_half(
+            half, got[0][half], inside, wt, wo, gb, zt, gating, sums, fact, send[1][half]
+        )
+        deliver(*forward(1, half))
+    product(1)
+    for half in range(2):
+        arrived(*backward(1, half))
+        last_half(half, got[1][half], inside, wo, gb, zt, gating, sums, o_ref)
+    for layer in range(2):
         for half in range(2):
-            for h in range(2):
-                recv[r, h, half] = got[half, 2 * r + h]
-        return carry
-
-    lax.fori_loop(0, DEV_ROWS, move, 0)
-    triangle(layer, begin_ref, extent_ref, recv, block_sums)
-    for half in range(2):
-        spread(member_ref, place_ref, block_sums, send.at[half], half)
-
-
-def k_middle(own_ref, got, zt_in, gating_in, wt, wo, gb, zt, gating, send, sums, fact):
-    inside = inside_mask(own_ref[0])
-    zt[...] = zt_in[...]
-    gating[...] = gating_in[...]
-    for half in range(2):
-        middle_half(half, got.at[half], inside, wt, wo, gb, zt, gating, sums, fact, send.at[half])
-
-
-def k_last(own_ref, got, zt, gating, wo, gb, o_ref, sums):
-    inside = inside_mask(own_ref[0])
-    for half in range(2):
-        last_half(half, got.at[half], inside, wo, gb, zt, gating, sums, o_ref)
+            others(*forward(layer, half)).wait_send()
+            others(*backward(layer, half)).wait_send()
 
 
 def body(pair_rep, token_counts, first_device, norm_gain, norm_bias, proj_weight, gate_weight, out_weight):
-    row = lax.axis_index("row")
-    extents = token_counts // ROWS
-    rows = jnp.arange(DEV_ROWS, dtype=jnp.int32)
-    member = jnp.sum((first_device[None, :] <= rows[:, None]).astype(jnp.int32), 1) - 1
-    place = rows - first_device[member]
-    own = extents[member[row]].reshape(1)
     smem = pl.BlockSpec(memory_space=pltpu.SMEM)
-    vmem = pl.BlockSpec(memory_space=pltpu.VMEM)
-    params = pltpu.CompilerParams(vmem_limit_bytes=48 * 2**20)
-    S = jax.ShapeDtypeStruct
-    zt_s, gating_s = S((ROWS, CH, CH), BF16), S((ROWS, CH, CH), F32)
-    send_s = S((2, DEVS, 2, HALF, CH), BF16)
-    back_s = S((2, DEVS, HALF, CH), BF16)
-    wt_s, wo_s, gb_s = S((2, 5 * CH, CH), BF16), S((2, CH, CH), BF16), S((2, 2, 2, CH, CH), F32)
-    fact_s = pltpu.VMEM((2, CH * HALF, CH), F32)
-    sums_s = pltpu.VMEM((CH * HALF, CH), F32)
-
-    def a2a(x):
-        return lax.all_to_all(x, ("row", "col"), 1, 1, tiled=True)
-
-    def tri(layer, got):
-        return pl.pallas_call(
-            functools.partial(k_triangle, layer),
-            out_shape=back_s,
-            in_specs=[smem] * 4 + [vmem],
-            out_specs=vmem,
-            scratch_shapes=[
-                pltpu.VMEM((DEV_ROWS + SPAN, 2, 2, 2, HALF, CH), BF16),
-                pltpu.VMEM((COMPLEXES, 2, 2, SPAN, HALF, CH), BF16),
-            ],
-            compiler_params=params,
-        )(first_device, extents, member, place, got)
-
-    zt, gating, send, wt, wo, gb = pl.pallas_call(
-        k_first,
-        out_shape=(zt_s, gating_s, send_s, wt_s, wo_s, gb_s),
-        in_specs=[smem] + [vmem] * 6,
-        out_specs=[vmem] * 6,
-        scratch_shapes=[fact_s],
-        compiler_params=params,
-    )(own, pair_rep, norm_gain, norm_bias, proj_weight, gate_weight, out_weight)
-    back = a2a(tri(0, a2a(send)))
-    zt, gating, send = pl.pallas_call(
-        k_middle,
-        out_shape=(zt_s, gating_s, send_s),
-        in_specs=[smem] + [vmem] * 6,
-        out_specs=[vmem] * 3,
-        scratch_shapes=[sums_s, fact_s],
-        compiler_params=params,
-    )(own, back, zt, gating, wt, wo, gb)
-    back = a2a(tri(1, a2a(send)))
+    anywhere = pl.BlockSpec(memory_space=pl.ANY)
+    loaded = (pair_rep, norm_gain, norm_bias, proj_weight, gate_weight, out_weight)
     return pl.pallas_call(
-        k_last,
-        out_shape=S((ROWS, CH, CH), BF16),
-        in_specs=[smem] + [vmem] * 5,
-        out_specs=vmem,
-        scratch_shapes=[sums_s],
-        compiler_params=params,
-    )(own, back, zt, gating, wo, gb)
+        kernel,
+        out_shape=jax.ShapeDtypeStruct(pair_rep.shape, BF16),
+        in_specs=[smem] * 2 + [anywhere] * 6,
+        out_specs=pl.BlockSpec(memory_space=pltpu.VMEM),
+        scratch_shapes=[pltpu.VMEM(a.shape, a.dtype) for a in loaded]
+        + [
+            pltpu.VMEM((2, 5 * CH, CH), BF16),
+            pltpu.VMEM((2, CH, CH), BF16),
+            pltpu.VMEM((2, 2, 2, CH, CH), F32),
+            pltpu.VMEM((ROWS, CH, CH), BF16),
+            pltpu.VMEM((ROWS, CH, CH), F32),
+            pltpu.VMEM((2, CH * HALF, CH), F32),
+            pltpu.VMEM((CH * HALF, CH), F32),
+            pltpu.VMEM((COMPLEXES, 2, 2, SPAN, HALF, CH), BF16),
+            pltpu.SemaphoreType.DMA((6,)),
+            pltpu.SemaphoreType.DMA((8,)),
+            pltpu.SemaphoreType.DMA((8,)),
+        ]
+        + [pltpu.VMEM((DEVS, 2, HALF, CH), BF16)] * 4
+        + [pltpu.VMEM((DEVS + 2 * SPAN, 2, HALF, CH), BF16)] * 4
+        + [pltpu.VMEM((DEVS, HALF, CH), BF16)] * 8,
+        compiler_params=pltpu.CompilerParams(
+            collective_id=0, has_side_effects=True, vmem_limit_bytes=56 * 2**20
+        ),
+        cost_estimate=pl.CostEstimate(
+            flops=3 * 10**9, bytes_accessed=16 * 2**20, transcendentals=6 * 2**20
+        ),
+    )(token_counts, first_device, *loaded)
 
 
 def solution(mesh):

time: 189 us -> 119 us (0.63)
  blocking collectives: 81.2 us -> 0 us
  Pallas kernels: 44.9 us -> 116 us
  waiting for transfers between devices: 29.1 us -> 0 us
  local copies, waits for them, and re-layouts: 17.5 us -> 2.31 us
  starting transfers between devices: 12 us -> 0 us
  between operations: 2.05 us -> 0.01 us
    all_to_all x3 -> x0, blocking collectives: 81.2 us -> none  [a2a(): return lax.all_to_all(x, ('row', 'col'), 1, 1, tiled=True)]
    pallas_call x5 -> x1, Pallas kernels: 44.9 us -> 116 us  [body(): pl.pallas_call(kernel, out_shape=jax.ShapeDtypeStruct(pair_rep.shape, BF1...]
    all_to_all x1 -> x0, waiting for transfers between devices: 29.1 us -> none  [a2a(): return lax.all_to_all(x, ('row', 'col'), 1, 1, tiled=True)]
    all_to_all x1 -> x0, starting transfers between devices: 12 us -> none  [a2a(): return lax.all_to_all(x, ('row', 'col'), 1, 1, tiled=True)]
    pallas_call x4 -> x0, local copies, waits for them, and re-layouts: 6.32 us -> none  [the longest x1 3.64 us: body(): pl.pallas_call(k_first, out_shape=(zt_s, gating_s, send_s, wt_s, wo_s, gb...]
    unnamed x16 -> x1, local copies, waits for them, and re-layouts: 6.56 us -> 2.31 us
    all_to_all x4 -> x0, local copies, waits for them, and re-layouts: 2.7 us -> none  [a2a(): return lax.all_to_all(x, ('row', 'col'), 1, 1, tiled=True)]
  transfers between devices with their start and end apart: 1 -> 0, of which waited for: 1 -> 0; matrix products, arithmetic and copies ran while one was open for 0% -> 0% of each run, Pallas kernels for 0% -> 0%
where the time goes in v2:
time: 119 us
  Pallas kernels  116 us (97%)
  local copies, waits for them, and re-layouts  2.31 us (2%)
    pallas_call x1, Pallas kernels, body(): pl.pallas_call(kernel, out_shape=jax.ShapeDtypeStruct(pair_rep.shape, BF1...  116 us

profile of v2, /device:TPU:1, one launch (start us, length us, event | category | flops | bytes accessed | tf_op | source)
XLA Modules:
  0.0 118.6 jit_solution(6552871484156524860)
XLA Ops:
  0.0 116.3 %shard_map.82 = bf16[32,128,128]{2,1,0:T(8,128)(2,1)} custom-call(s32[16]{0:T(128)} %count_ref.1, s32[16]{0:T(128)} %begin_ref.1, bf16[32,128,128]{2,1,0:T(8,128)(2,1)} %z_hbm.1, f32[2,2,128]{2,1,0:T(2,128)} %gain_hbm.1, f32[2,2,128]{2,1,0:T(2,128)} %bias_hbm.1, bf16[2,128,512]{2,1,0:T(8,128)(2,1)} %proj_hbm.1, bf16[2,128,128]{2,1,0:T(8,128)(2,1)} %gate_hbm.1, ...), custom_call_target="tpu_custom_call" | custom-call | flops 3000000000 | bytes 16777216 | tf_op jit(solution)/shard_map/pallas_call | solution.py:316
  116.3 2.3 %copy.10 = bf16[32,128,128]{2,1,0:T(8,128)(2,1)} copy(bf16[32,128,128]{2,1,0:T(8,128)(2,1)} %shard_map.82) | data formatting | bytes 2097152

commit v3 on v2

--- a/solution.py
+++ b/solution.py
@@ -68,7 +68,7 @@
     def step(t, carry):
         for f in range(2):
             block = fact[f, pl.ds(pl.multiple_of(t * 256, 256), 256), :]
-            send[pl.ds(t * 16, 16), f] = block.reshape(16, HALF, CH).astype(BF16)
+            send[f][pl.ds(t * 16, 16)] = block.reshape(16, HALF, CH).astype(BF16)
         return carry
 
     lax.fori_loop(0, 8, step, 0)
@@ -143,36 +143,62 @@
     lax.fori_loop(0, HALF // 2, step, 0)
 
 
-def triangle(layer, begin_ref, count_ref, recv, block_sums):
-    dims = (((1,), (1,)), ((), ())) if layer == 0 else (((0,), (0,)), ((), ()))
-
+def window(ref, begin, ours, cores=(0, 1)):
+    part = ref[pl.ds(2 * begin, 2 * SPAN)].reshape(SPAN, 2, HALF, CH)
+    return jnp.concatenate(
+        [jnp.where(ours, part[:, h], jnp.zeros((), BF16)).reshape(CH, CH) for h in cores], axis=1
+    )
+
+
+def per_complex(begin_ref, count_ref, work):
     def step(b, carry):
         begin = jnp.clip(begin_ref[b], 0, DEV_ROWS - 1)
         ours = lax.broadcasted_iota(jnp.int32, (SPAN, HALF, CH), 0) * ROWS < count_ref[b]
-
-        parts = [
-            recv[half][pl.ds(2 * begin, 2 * SPAN)].reshape(SPAN, 2, 2, HALF, CH) for half in range(2)
-        ]
-
-        def window(f):
-            tall = []
-            for half in range(2):
-                wide = [
-                    jnp.where(ours, parts[half][:, h, f], jnp.zeros((), BF16)).reshape(CH, CH)
-                    for h in range(2)
-                ]
-                tall.append(jnp.concatenate(wide, axis=1))
-            return jnp.concatenate(tall, axis=0)
-
-        s = lax.dot_general(window(0), window(1), dims, preferred_element_type=F32).astype(BF16)
-        for hi in range(2):
-            for hj in range(2):
-                block_sums[b, hj, hi] = s[hi * CH : (hi + 1) * CH, hj * CH : (hj + 1) * CH].reshape(
-                    SPAN, HALF, CH
-                )
+        work(b, begin, ours)
         return carry
 
     lax.fori_loop(0, COMPLEXES, step, 0)
+
+
+def keep(block_sums, b, sums):
+    for core in range(2):
+        block_sums[b, core] = sums[:, core * CH : (core + 1) * CH].astype(BF16).reshape(SPAN, HALF, CH)
+
+
+def outgoing(begin_ref, count_ref, left, right, block_sums):
+    def work(b, begin, ours):
+        them = jnp.concatenate([window(ref, begin, ours) for ref in right], axis=0)
+        sums = lax.dot_general(
+            window(left, begin, ours), them, (((1,), (1,)), ((), ())), preferred_element_type=F32
+        )
+        keep(block_sums, b, sums)
+
+    per_complex(begin_ref, count_ref, work)
+
+
+def incoming_start(begin_ref, count_ref, left, right, partial):
+    def work(b, begin, ours):
+        partial[b] = lax.dot_general(
+            window(left, begin, ours),
+            window(right, begin, ours),
+            (((0,), (0,)), ((), ())),
+            preferred_element_type=F32,
+        )
+
+    per_complex(begin_ref, count_ref, work)
+
+
+def incoming_end(begin_ref, count_ref, left, right, partial, core, block_sums):
+    def work(b, begin, ours):
+        sums = partial[b, core * CH : (core + 1) * CH] + lax.dot_general(
+            window(left, begin, ours, (core,)),
+            window(right, begin, ours),
+            (((0,), (0,)), ((), ())),
+            preferred_element_type=F32,
+        )
+        keep(block_sums, b, sums)
+
+    per_complex(begin_ref, count_ref, work)
 
 
 def spread(begin_ref, block_sums, send):
@@ -180,9 +206,8 @@
         later = jnp.minimum(b + 1, COMPLEXES - 1)
         b = jnp.where(begin_ref[later] <= r, later, b)
         q = jnp.clip(r - begin_ref[b], 0, SPAN - 1)
-        for half in range(2):
-            for hj in range(2):
-                send[half][2 * r + hj] = block_sums[b, hj, half, q]
+        for core in range(2):
+            send[2 * r + core] = block_sums[b, core, q]
         return b
 
     lax.fori_loop(0, DEV_ROWS, step, jnp.int32(0))
@@ -199,18 +224,28 @@
     count_ref, begin_ref, z_hbm, gain_hbm, bias_hbm, proj_hbm, gate_hbm, outw_hbm,
     o_ref,
     z_ref, gain_ref, bias_ref, proj_ref, gate_ref, outw_ref,
-    wt, wo, gb, zt, gating, fact, sums, block_sums, load_sem, send_sem, recv_sem, *exchanged,
+    wt, wo, gb, zt, gating, fact, sums, block_sums, partial, load_sem, send_sem, recv_sem, *exchanged,
 ):
-    send, recv, back, got = [
-        [exchanged[k : k + 2], exchanged[k + 2 : k + 4]] for k in range(0, 16, 4)
-    ]
+    send, recv, back, got = exchanged[:5], exchanged[5:10], exchanged[10:14], exchanged[14:18]
     row, col = lax.axis_index("row"), lax.axis_index("col")
     me = row * 2 + col
-    y, x, z = row // 16, (row // 4) % 4, row % 4
-
-    def peer(s):
-        to = ((y + s // 32) % 4) * 16 + ((x + (s // 8) % 4) % 4) * 4 + (z + (s // 2) % 4) % 4
-        return to, (col + s) % 2
+    y, x, z = row >> 4, (row >> 2) & 3, row & 3
+    planes = [((y + dy) & 3) * 16 for dy in range(4)]
+    cores = (col, 1 - col)
+
+    def peers(work):
+        def group(t, first):
+            for dy in range(4):
+                to = planes[dy] + ((x + (t >> 2) + dy) & 3) * 4 + ((z + t + dy) & 3)
+                for core in cores[first:] if dy == 0 else cores:
+                    work(to, core)
+
+        def step(t, carry):
+            group(t, 0)
+            return carry
+
+        group(0, 1)
+        lax.fori_loop(1, 16, step, 0)
 
     loads = [
         pltpu.make_async_copy(src, dst, load_sem.at[k])
@@ -228,16 +263,16 @@
     for load in loads:
         load.start()
 
-    for ref in recv[0] + recv[1]:
+    for ref in recv:
         ref[pl.ds(DEVS, 2 * SPAN)] = jnp.zeros((2 * SPAN,) + ref.shape[1:], BF16)
 
     barrier = pltpu.get_barrier_semaphore()
 
-    def greet(s, carry):
-        pl.semaphore_signal(barrier, inc=1, device_id=peer(s), device_id_type=MESH)
-        return carry
-
-    lax.fori_loop(1, DEVS, greet, 0)
+    peers(
+        lambda to, core: pl.semaphore_signal(
+            barrier, inc=1, device_id=(to, core), device_id_type=MESH
+        )
+    )
 
     inside = inside_mask(row, begin_ref, count_ref)
     for load in loads:
@@ -245,8 +280,7 @@
     prepare(gain_ref, bias_ref, proj_ref, gate_ref, outw_ref, wt, wo, gb)
 
     def deliver(src, dst, k):
-        def step(s, carry):
-            to, core = peer((s * 37) % DEVS)
+        def copy(to, core):
             pltpu.make_async_remote_copy(
                 src_ref=src.at[to * 2 + core],
                 dst_ref=dst.at[me],
@@ -255,9 +289,8 @@
                 device_id=(to, core),
                 device_id_type=MESH,
             ).start()
-            return carry
-
-        lax.fori_loop(1, DEVS, step, 0)
+
+        peers(copy)
 
     def others(src, dst, k):
         return pltpu.make_async_remote_copy(
@@ -273,45 +306,63 @@
         others(src, dst, k).wait_recv()
         dst[me] = src[me]
 
-    def forward(layer, half):
-        return send[layer][half], recv[layer][half], 4 * layer + half
-
-    def backward(layer, half):
-        return back[layer][half], got[layer][half], 4 * layer + 2 + half
-
-    def product(layer):
-        for half in range(2):
-            arrived(*forward(layer, half))
-        triangle(layer, begin_ref, count_ref, recv[layer], block_sums)
-        spread(begin_ref, block_sums, back[layer])
-        for half in range(2):
-            deliver(*backward(layer, half))
+    def forward(k):
+        return send[k], recv[k], k
+
+    def backward(k):
+        return back[k], got[k], 5 + k
+
+    def factors(refs, k):
+        return [refs[k].at[:, f] for f in range(2)]
+
+    def to_back(k):
+        spread(begin_ref, block_sums, back[k])
+        deliver(*backward(k))
+
+    first_half(0, z_ref, inside, wt, gb, zt, gating, fact, factors(send, 0))
+    pl.semaphore_wait(barrier, DEVS - 1)
+    deliver(*forward(0))
+    first_half(1, z_ref, inside, wt, gb, zt, gating, fact, (send[2], send[1]))
+    deliver(*forward(1))
+    deliver(*forward(2))
+
+    arrived(*forward(0))
+    arrived(*forward(1))
+    left, right = factors(recv, 0)
+    outgoing(begin_ref, count_ref, left, (right, recv[1]), block_sums)
+    to_back(0)
+    arrived(*forward(2))
+    outgoing(begin_ref, count_ref, recv[2], (right, recv[1]), block_sums)
+    to_back(1)
 
     for half in range(2):
-        first_half(half, z_ref, inside, wt, gb, zt, gating, fact, send[0][half])
-        if half == 0:
-            pl.semaphore_wait(barrier, DEVS - 1)
-        deliver(*forward(0, half))
-    product(0)
+        arrived(*backward(half))
+        middle_half(
+            half, got[half], inside, wt, wo, gb, zt, gating, sums, fact, factors(send, 3 + half)
+        )
+        deliver(*forward(3 + half))
+
+    arrived(*forward(3))
+    incoming_start(begin_ref, count_ref, *factors(recv, 3), partial)
+    arrived(*forward(4))
+    for core in range(2):
+        incoming_end(begin_ref, count_ref, *factors(recv, 4), partial, core, block_sums)
+        to_back(2 + core)
+
     for half in range(2):
-        arrived(*backward(0, half))
-        middle_half(
-            half, got[0][half], inside, wt, wo, gb, zt, gating, sums, fact, send[1][half]
-        )
-        deliver(*forward(1, half))
-    product(1)
-    for half in range(2):
-        arrived(*backward(1, half))
-        last_half(half, got[1][half], inside, wo, gb, zt, gating, sums, o_ref)
-    for layer in range(2):
-        for half in range(2):
-            others(*forward(layer, half)).wait_send()
-            others(*backward(layer, half)).wait_send()
+        arrived(*backward(2 + half))
+        last_half(half, got[2 + half], inside, wo, gb, zt, gating, sums, o_ref)
+    for k in range(5):
+        others(*forward(k)).wait_send()
+    for k in range(4):
+        others(*backward(k)).wait_send()
 
 
 def body(pair_rep, token_counts, first_device, norm_gain, norm_bias, proj_weight, gate_weight, out_weight):
     smem = pl.BlockSpec(memory_space=pltpu.SMEM)
     anywhere = pl.BlockSpec(memory_space=pl.ANY)
+    both, one = (2, HALF, CH), (HALF, CH)
+    forms = (both, one, one, both, both)
     loaded = (pair_rep, norm_gain, norm_bias, proj_weight, gate_weight, out_weight)
     return pl.pallas_call(
         kernel,
@@ -327,13 +378,14 @@
             pltpu.VMEM((ROWS, CH, CH), F32),
             pltpu.VMEM((2, CH * HALF, CH), F32),
             pltpu.VMEM((CH * HALF, CH), F32),
-            pltpu.VMEM((COMPLEXES, 2, 2, SPAN, HALF, CH), BF16),
+            pltpu.VMEM((COMPLEXES, 2, SPAN, HALF, CH), BF16),
+            pltpu.VMEM((COMPLEXES, 2 * CH, 2 * CH), F32),
             pltpu.SemaphoreType.DMA((6,)),
-            pltpu.SemaphoreType.DMA((8,)),
-            pltpu.SemaphoreType.DMA((8,)),
+            pltpu.SemaphoreType.DMA((9,)),
+            pltpu.SemaphoreType.DMA((9,)),
         ]
-        + [pltpu.VMEM((DEVS, 2, HALF, CH), BF16)] * 4
-        + [pltpu.VMEM((DEVS + 2 * SPAN, 2, HALF, CH), BF16)] * 4
+        + [pltpu.VMEM((DEVS,) + form, BF16) for form in forms]
+        + [pltpu.VMEM((DEVS + 2 * SPAN,) + form, BF16) for form in forms]
         + [pltpu.VMEM((DEVS, HALF, CH), BF16)] * 8,
         compiler_params=pltpu.CompilerParams(
             collective_id=0, has_side_effects=True, vmem_limit_bytes=56 * 2**20

time: 119 us -> 110 us (0.924)
  Pallas kernels: 116 us -> 108 us
    pallas_call x1, Pallas kernels: 116 us -> 108 us  [body(): pl.pallas_call(kernel, out_shape=jax.ShapeDtypeStruct(pair_rep.shape, BF1...]
where the time goes in v3:
time: 110 us
  Pallas kernels  108 us (98%)
  local copies, waits for them, and re-layouts  2.31 us (2%)
    pallas_call x1, Pallas kernels, body(): pl.pallas_call(kernel, out_shape=jax.ShapeDtypeStruct(pair_rep.shape, BF1...  108 us
    unnamed x1, local copies, waits for them, and re-layouts  2.31 us

profile of v3, /device:TPU:1, one launch (start us, length us, event | category | flops | bytes accessed | tf_op | source)
XLA Modules:
  0.0 110.2 jit_solution(3173619168387658738)
XLA Ops:
  0.0 107.9 %shard_map.82 = bf16[32,128,128]{2,1,0:T(8,128)(2,1)} custom-call(s32[16]{0:T(128)} %count_ref.1, s32[16]{0:T(128)} %begin_ref.1, bf16[32,128,128]{2,1,0:T(8,128)(2,1)} %z_hbm.1, f32[2,2,128]{2,1,0:T(2,128)} %gain_hbm.1, f32[2,2,128]{2,1,0:T(2,128)} %bias_hbm.1, bf16[2,128,512]{2,1,0:T(8,128)(2,1)} %proj_hbm.1, bf16[2,128,128]{2,1,0:T(8,128)(2,1)} %gate_hbm.1, ...), custom_call_target="tpu_custom_call" | custom-call | flops 3000000000 | bytes 16777216 | tf_op jit(solution)/shard_map/pallas_call | solution.py:367
  107.9 2.3 %copy.10 = bf16[32,128,128]{2,1,0:T(8,128)(2,1)} copy(bf16[32,128,128]{2,1,0:T(8,128)(2,1)} %shard_map.82) | data formatting | bytes 2097152

commit v4 on v3

--- a/solution.py
+++ b/solution.py
@@ -71,7 +71,7 @@
             send[f][pl.ds(t * 16, 16)] = block.reshape(16, HALF, CH).astype(BF16)
         return carry
 
-    lax.fori_loop(0, 8, step, 0)
+    lax.fori_loop(0, 8, step, 0, unroll=4)
 
 
 def first_half(half, z_ref, inside, wt, gb, zt, gating, fact, send):
@@ -84,7 +84,7 @@
         project(0, pair, i, inside, wt, gb, gating.at[pl.ds(row, 2)], fact)
         return carry
 
-    lax.fori_loop(0, HALF // 2, step, 0)
+    lax.fori_loop(0, HALF // 2, step, 0, unroll=4)
     pack(fact, send)
 
 
@@ -108,7 +108,7 @@
         sums[pl.ds(pl.multiple_of(t * 256, 256), 256), :] = block.reshape(256, CH)
         return carry
 
-    lax.fori_loop(0, 8, step, 0)
+    lax.fori_loop(0, 8, step, 0, unroll=4)
 
 
 def middle_half(half, got, inside, wt, wo, gb, zt, gating, sums, fact, send):
@@ -125,7 +125,7 @@
         )
         return carry
 
-    lax.fori_loop(0, HALF // 2, step, 0)
+    lax.fori_loop(0, HALF // 2, step, 0, unroll=4)
     pack(fact, send)
 
 
@@ -140,24 +140,26 @@
             o_ref[row + e] = flip(pair[e]).astype(BF16)
         return carry
 
-    lax.fori_loop(0, HALF // 2, step, 0)
-
-
-def window(ref, begin, ours, cores=(0, 1)):
+    lax.fori_loop(0, HALF // 2, step, 0, unroll=4)
+
+
+def window(ref, begin, count=None, cores=(0, 1)):
     part = ref[pl.ds(2 * begin, 2 * SPAN)].reshape(SPAN, 2, HALF, CH)
-    return jnp.concatenate(
-        [jnp.where(ours, part[:, h], jnp.zeros((), BF16)).reshape(CH, CH) for h in cores], axis=1
-    )
+    tall = []
+    for q in range(SPAN):
+        wide = jnp.concatenate([part[q, h] for h in cores], axis=1)
+        if count is not None and q >= 2:
+            wide = jnp.where(q * ROWS < count, wide, jnp.zeros_like(wide))
+        tall.append(wide)
+    return jnp.concatenate(tall, axis=0)
 
 
 def per_complex(begin_ref, count_ref, work):
     def step(b, carry):
-        begin = jnp.clip(begin_ref[b], 0, DEV_ROWS - 1)
-        ours = lax.broadcasted_iota(jnp.int32, (SPAN, HALF, CH), 0) * ROWS < count_ref[b]
-        work(b, begin, ours)
-        return carry
-
-    lax.fori_loop(0, COMPLEXES, step, 0)
+        work(b, jnp.clip(begin_ref[b], 0, DEV_ROWS - 1), count_ref[b])
+        return carry
+
+    lax.fori_loop(0, COMPLEXES, step, 0, unroll=8)
 
 
 def keep(block_sums, b, sums):
@@ -166,10 +168,10 @@
 
 
 def outgoing(begin_ref, count_ref, left, right, block_sums):
-    def work(b, begin, ours):
-        them = jnp.concatenate([window(ref, begin, ours) for ref in right], axis=0)
+    def work(b, begin, count):
+        them = jnp.concatenate([window(ref, begin, count) for ref in right], axis=0)
         sums = lax.dot_general(
-            window(left, begin, ours), them, (((1,), (1,)), ((), ())), preferred_element_type=F32
+            window(left, begin), them, (((1,), (1,)), ((), ())), preferred_element_type=F32
         )
         keep(block_sums, b, sums)
 
@@ -177,10 +179,10 @@
 
 
 def incoming_start(begin_ref, count_ref, left, right, partial):
-    def work(b, begin, ours):
+    def work(b, begin, count):
         partial[b] = lax.dot_general(
-            window(left, begin, ours),
-            window(right, begin, ours),
+            window(left, begin),
+            window(right, begin, count),
             (((0,), (0,)), ((), ())),
             preferred_element_type=F32,
         )
@@ -189,10 +191,10 @@
 
 
 def incoming_end(begin_ref, count_ref, left, right, partial, core, block_sums):
-    def work(b, begin, ours):
+    def work(b, begin, count):
         sums = partial[b, core * CH : (core + 1) * CH] + lax.dot_general(
-            window(left, begin, ours, (core,)),
-            window(right, begin, ours),
+            window(left, begin, None, (core,)),
+            window(right, begin, count),
             (((0,), (0,)), ((), ())),
             preferred_element_type=F32,
         )
@@ -210,7 +212,7 @@
             send[2 * r + core] = block_sums[b, core, q]
         return b
 
-    lax.fori_loop(0, DEV_ROWS, step, jnp.int32(0))
+    lax.fori_loop(0, DEV_ROWS, step, jnp.int32(0), unroll=16)
 
 
 def inside_mask(row, begin_ref, count_ref):

time: 110 us -> 99.6 us (0.905)
  Pallas kernels: 108 us -> 97.1 us
    pallas_call x1, Pallas kernels: 108 us -> 97.1 us  [body(): pl.pallas_call(kernel, out_shape=jax.ShapeDtypeStruct(pair_rep.shape, BF1...]
where the time goes in v4:
time: 99.6 us; the launch traced here: 99.4 us
  Pallas kernels  97.1 us (97%)
  local copies, waits for them, and re-layouts  2.31 us (2%)
    pallas_call x1, Pallas kernels, body(): pl.pallas_call(kernel, out_shape=jax.ShapeDtypeStruct(pair_rep.shape, BF1...  97.1 us
    unnamed x1, local copies, waits for them, and re-layouts  2.31 us

profile of v4, /device:TPU:1, one launch (start us, length us, event | category | flops | bytes accessed | tf_op | source)
XLA Modules:
  0.0 99.4 jit_solution(1842966566113539645)
XLA Ops:
  0.0 97.1 %shard_map.82 = bf16[32,128,128]{2,1,0:T(8,128)(2,1)} custom-call(s32[16]{0:T(128)} %count_ref.1, s32[16]{0:T(128)} %begin_ref.1, bf16[32,128,128]{2,1,0:T(8,128)(2,1)} %z_hbm.1, f32[2,2,128]{2,1,0:T(2,128)} %gain_hbm.1, f32[2,2,128]{2,1,0:T(2,128)} %bias_hbm.1, bf16[2,128,512]{2,1,0:T(8,128)(2,1)} %proj_hbm.1, bf16[2,128,128]{2,1,0:T(8,128)(2,1)} %gate_hbm.1, ...), custom_call_target="tpu_custom_call" | custom-call | flops 3000000000 | bytes 16777216 | tf_op jit(solution)/shard_map/pallas_call | solution.py:369
  97.1 2.3 %copy.10 = bf16[32,128,128]{2,1,0:T(8,128)(2,1)} copy(bf16[32,128,128]{2,1,0:T(8,128)(2,1)} %shard_map.82) | data formatting | bytes 2097152

commit v5 on v4

--- a/solution.py
+++ b/solution.py
@@ -71,7 +71,7 @@
             send[f][pl.ds(t * 16, 16)] = block.reshape(16, HALF, CH).astype(BF16)
         return carry
 
-    lax.fori_loop(0, 8, step, 0, unroll=4)
+    lax.fori_loop(0, 8, step, 0, unroll=8)
 
 
 def first_half(half, z_ref, inside, wt, gb, zt, gating, fact, send):
@@ -84,7 +84,7 @@
         project(0, pair, i, inside, wt, gb, gating.at[pl.ds(row, 2)], fact)
         return carry
 
-    lax.fori_loop(0, HALF // 2, step, 0, unroll=4)
+    lax.fori_loop(0, HALF // 2, step, 0, unroll=8)
     pack(fact, send)
 
 
@@ -108,7 +108,7 @@
         sums[pl.ds(pl.multiple_of(t * 256, 256), 256), :] = block.reshape(256, CH)
         return carry
 
-    lax.fori_loop(0, 8, step, 0, unroll=4)
+    lax.fori_loop(0, 8, step, 0, unroll=8)
 
 
 def middle_half(half, got, inside, wt, wo, gb, zt, gating, sums, fact, send):
@@ -125,7 +125,7 @@
         )
         return carry
 
-    lax.fori_loop(0, HALF // 2, step, 0, unroll=4)
+    lax.fori_loop(0, HALF // 2, step, 0, unroll=8)
     pack(fact, send)
 
 
@@ -140,7 +140,7 @@
             o_ref[row + e] = flip(pair[e]).astype(BF16)
         return carry
 
-    lax.fori_loop(0, HALF // 2, step, 0, unroll=4)
+    lax.fori_loop(0, HALF // 2, step, 0, unroll=8)
 
 
 def window(ref, begin, count=None, cores=(0, 1)):

time: 99.6 us -> 98.8 us (level)
  no operation moved by 1% of the time
where the time goes in v5:
time: 98.8 us; the launch traced here: 98.7 us
  Pallas kernels  96.3 us (97%)
  local copies, waits for them, and re-layouts  2.31 us (2%)
    pallas_call x1, Pallas kernels, body(): pl.pallas_call(kernel, out_shape=jax.ShapeDtypeStruct(pair_rep.shape, BF1...  96.3 us
    unnamed x1, local copies, waits for them, and re-layouts  2.31 us

profile of v5, /device:TPU:1, one launch (start us, length us, event | category | flops | bytes accessed | tf_op | source)
XLA Modules:
  0.0 98.7 jit_solution(14370020338349681707)
XLA Ops:
  0.0 96.3 %shard_map.82 = bf16[32,128,128]{2,1,0:T(8,128)(2,1)} custom-call(s32[16]{0:T(128)} %count_ref.1, s32[16]{0:T(128)} %begin_ref.1, bf16[32,128,128]{2,1,0:T(8,128)(2,1)} %z_hbm.1, f32[2,2,128]{2,1,0:T(2,128)} %gain_hbm.1, f32[2,2,128]{2,1,0:T(2,128)} %bias_hbm.1, bf16[2,128,512]{2,1,0:T(8,128)(2,1)} %proj_hbm.1, bf16[2,128,128]{2,1,0:T(8,128)(2,1)} %gate_hbm.1, ...), custom_call_target="tpu_custom_call" | custom-call | flops 3000000000 | bytes 16777216 | tf_op jit(solution)/shard_map/pallas_call | solution.py:369
  96.3 2.3 %copy.10 = bf16[32,128,128]{2,1,0:T(8,128)(2,1)} copy(bf16[32,128,128]{2,1,0:T(8,128)(2,1)} %shard_map.82) | data formatting | bytes 2097152

commit v6 on v5

--- a/solution.py
+++ b/solution.py
@@ -378,8 +378,8 @@
             pltpu.VMEM((2, 2, 2, CH, CH), F32),
             pltpu.VMEM((ROWS, CH, CH), BF16),
             pltpu.VMEM((ROWS, CH, CH), F32),
-            pltpu.VMEM((2, CH * HALF, CH), F32),
-            pltpu.VMEM((CH * HALF, CH), F32),
+            pltpu.VMEM((2, CH * HALF + HALF, CH), F32),
+            pltpu.VMEM((CH * HALF + HALF, CH), F32),
             pltpu.VMEM((COMPLEXES, 2, SPAN, HALF, CH), BF16),
             pltpu.VMEM((COMPLEXES, 2 * CH, 2 * CH), F32),
             pltpu.SemaphoreType.DMA((6,)),

time: 98.8 us -> 98.7 us (level)
  no operation moved by 1% of the time
where the time goes in v6:
time: 98.7 us; the launch traced here: 98.6 us
  Pallas kernels  96.3 us (98%)
  local copies, waits for them, and re-layouts  2.31 us (2%)
    pallas_call x1, Pallas kernels, body(): pl.pallas_call(kernel, out_shape=jax.ShapeDtypeStruct(pair_rep.shape, BF1...  96.3 us
    unnamed x1, local copies, waits for them, and re-layouts  2.31 us

profile of v6, /device:TPU:1, one launch (start us, length us, event | category | flops | bytes accessed | tf_op | source)
XLA Modules:
  0.0 98.6 jit_solution(1021840049949124431)
XLA Ops:
  0.0 96.3 %shard_map.82 = bf16[32,128,128]{2,1,0:T(8,128)(2,1)} custom-call(s32[16]{0:T(128)} %count_ref.1, s32[16]{0:T(128)} %begin_ref.1, bf16[32,128,128]{2,1,0:T(8,128)(2,1)} %z_hbm.1, f32[2,2,128]{2,1,0:T(2,128)} %gain_hbm.1, f32[2,2,128]{2,1,0:T(2,128)} %bias_hbm.1, bf16[2,128,512]{2,1,0:T(8,128)(2,1)} %proj_hbm.1, bf16[2,128,128]{2,1,0:T(8,128)(2,1)} %gate_hbm.1, ...), custom_call_target="tpu_custom_call" | custom-call | flops 3000000000 | bytes 16777216 | tf_op jit(solution)/shard_map/pallas_call | solution.py:369
  96.3 2.3 %copy.10 = bf16[32,128,128]{2,1,0:T(8,128)(2,1)} copy(bf16[32,128,128]{2,1,0:T(8,128)(2,1)} %shard_map.82) | data formatting | bytes 2097152

commit v7 on v6

--- a/solution.py
+++ b/solution.py
@@ -247,7 +247,7 @@
             return carry
 
         group(0, 1)
-        lax.fori_loop(1, 16, step, 0)
+        lax.fori_loop(1, 16, step, 0, unroll=3)
 
     loads = [
         pltpu.make_async_copy(src, dst, load_sem.at[k])

time: 98.7 us -> 98.9 us (level)
  no operation moved by 1% of the time
where the time goes in v7:
time: 98.9 us; the launch traced here: 98.8 us
  Pallas kernels  96.5 us (98%)
  local copies, waits for them, and re-layouts  2.31 us (2%)
    pallas_call x1, Pallas kernels, body(): pl.pallas_call(kernel, out_shape=jax.ShapeDtypeStruct(pair_rep.shape, BF1...  96.5 us
    unnamed x1, local copies, waits for them, and re-layouts  2.31 us

profile of v7, /device:TPU:1, one launch (start us, length us, event | category | flops | bytes accessed | tf_op | source)
XLA Modules:
  0.0 98.8 jit_solution(11122249399048730851)
XLA Ops:
  0.0 96.5 %shard_map.82 = bf16[32,128,128]{2,1,0:T(8,128)(2,1)} custom-call(s32[16]{0:T(128)} %count_ref.1, s32[16]{0:T(128)} %begin_ref.1, bf16[32,128,128]{2,1,0:T(8,128)(2,1)} %z_hbm.1, f32[2,2,128]{2,1,0:T(2,128)} %gain_hbm.1, f32[2,2,128]{2,1,0:T(2,128)} %bias_hbm.1, bf16[2,128,512]{2,1,0:T(8,128)(2,1)} %proj_hbm.1, bf16[2,128,128]{2,1,0:T(8,128)(2,1)} %gate_hbm.1, ...), custom_call_target="tpu_custom_call" | custom-call | flops 3000000000 | bytes 16777216 | tf_op jit(solution)/shard_map/pallas_call | solution.py:369
  96.5 2.3 %copy.10 = bf16[32,128,128]{2,1,0:T(8,128)(2,1)} copy(bf16[32,128,128]{2,1,0:T(8,128)(2,1)} %shard_map.82) | data formatting | bytes 2097152
